TPU v7x, 256 devices: a whole 4x4x8 slice. The times are simulated.
256 devices in a mesh: row: 32 (over x_hi, z, core), col: 8 (over x_lo, y).
Axes of the slice: x: 4 (x_hi: 2, x_lo: 2; x = x_hi * 2 + x_lo), y: 4, z: 8, core: 2. Of those that a mesh axis runs over, the one named last changes fastest.
Arguments:
- queries: bfloat16 [131072, 256], P(('row', 'col')), may hold values from -36 to 36
- key_rows: bfloat16 [131072, 128], P(('row', 'col')), may hold values from -16 to 16
- value_rows: bfloat16 [131072, 128], P(('row', 'col')), may hold values from -6 to 6
- out_grad: bfloat16 [131072, 256], P(('row', 'col')), may hold values from -6 to 6
- link_mask: int32 [256, 5], P(('row', 'col')), may hold values 0 or 1
Outputs:
- attention_out: bfloat16 [131072, 256], P(('row', 'col'))
- query_grad: bfloat16 [131072, 256], P(('row', 'col'))
- key_grad: bfloat16 [131072, 128], P(('row', 'col'))
- value_grad: bfloat16 [131072, 128], P(('row', 'col'))
All inputs are finite; a program needn't handle non-finite values. No bound on the sum of `link_mask` on one device may be relied on, other than what follows from the above.
Results may differ from a plain program's by a relative error of at most 0.025.
Values may be sent and summed in bfloat16 or wider, within the bound.
A program may use at most 64 MiB of HBM per device.

v0:
```python
import math

import jax
import jax.numpy as jnp
from jax import lax
from jax.sharding import PartitionSpec as P

scale_eps = 1e-06


def shifted(value, axis, steps):
    count = lax.axis_size(axis)
    leading, last = (max(0, -steps), min(count, count - steps))
    return lax.ppermute(value, axis, [(source, source + steps) for source in range(leading, last)])


def quantize(values):
    largest = jnp.max(jnp.abs(values), axis=-1)
    scales = (largest + scale_eps).astype(jnp.bfloat16)
    scaled = values * (127.0 / scales.astype(jnp.float32))[..., None]
    codes = jnp.clip(jnp.floor(scaled + 0.5), -127.0, 127.0).astype(jnp.bfloat16)
    return (codes, scales)


def dequantize(codes, scales):
    return (codes.astype(jnp.float32) * (scales.astype(jnp.float32) / 127.0)[..., None]).astype(
        jnp.bfloat16
    )


def score_block(query_codes, query_scales, key_codes, key_scales):
    head_size = key_codes.shape[-1]
    factor = 1.0 / (127.0 * 127.0 * math.sqrt(head_size))
    raw = jnp.einsum("thc,uc->htu", query_codes, key_codes, preferred_element_type=jnp.float32)
    row_factor = jnp.transpose(query_scales.astype(jnp.float32) * factor)
    return raw * row_factor[:, :, None] * key_scales.astype(jnp.float32)[None, None, :]


def fetch_keys(bundle, distance):
    return shifted((bundle[0], bundle[1], bundle[2]), ("row", "col"), distance)


def return_grads(partials):
    levels_count = len(partials)
    key_back = jnp.zeros_like(partials[0][0])
    value_back = jnp.zeros_like(partials[0][1])
    for level in range(levels_count):
        arrived = shifted(partials[level], ("row", "col"), -(2**level))
        key_back = key_back + arrived[0]
        value_back = value_back + arrived[1]
    return (key_back, value_back)


def local(queries, key_rows, value_rows, out_grad, link_mask):
    tokens_dev = queries.shape[0]
    head_size = key_rows.shape[1]
    heads_count = queries.shape[1] // head_size
    levels_count = link_mask.shape[1]
    score_scale = 1.0 / math.sqrt(head_size)
    query_float = queries.astype(jnp.float32).reshape(tokens_dev, heads_count, head_size)
    query_codes, query_scales = quantize(query_float)
    query_hat = dequantize(query_codes, query_scales)
    key_codes, key_scales = quantize(key_rows.astype(jnp.float32))
    grad_three = out_grad.reshape(tokens_dev, heads_count, head_size)
    grad_float = grad_three.astype(jnp.float32)
    block_id = lax.axis_index(("row", "col"))
    positions = jnp.arange(tokens_dev, dtype=jnp.int32)
    causal = (positions[None, :] <= positions[:, None])[None, :, :]
    sources = [((key_codes, key_scales, value_rows), causal)]
    for level in range(levels_count):
        distance = 2**level
        fetched = fetch_keys((key_codes, key_scales, value_rows), distance)
        allowed = jnp.logical_and(block_id >= distance, link_mask[0, level] == 1)
        sources.append((fetched, allowed))

    def masked_scores(bundle, allowed):
        return jnp.where(
            allowed, score_block(query_codes, query_scales, bundle[0], bundle[1]), -jnp.inf
        )

    row_top = None
    for bundle, allowed in sources:
        current = jnp.max(masked_scores(bundle, allowed), axis=2)
        row_top = current if row_top is None else jnp.maximum(row_top, current)
    total = jnp.zeros((heads_count, tokens_dev), jnp.float32)
    mixed = jnp.zeros((tokens_dev, heads_count, head_size), jnp.float32)
    for bundle, allowed in sources:
        weights = jnp.exp(masked_scores(bundle, allowed) - row_top[:, :, None])
        total = total + jnp.sum(weights, axis=2)
        mixed = mixed + jnp.einsum(
            "htu,uc->thc",
            weights.astype(jnp.bfloat16),
            bundle[2],
            preferred_element_type=jnp.float32,
        )
    attended = (mixed / jnp.transpose(total)[:, :, None]).astype(jnp.bfloat16)
    delta = jnp.sum(grad_float * attended.astype(jnp.float32), axis=2)
    query_sum = jnp.zeros((tokens_dev, heads_count, head_size), jnp.float32)
    partials = []
    own_part = None
    for position, (bundle, allowed) in enumerate(sources):
        weights = jnp.exp(masked_scores(bundle, allowed) - row_top[:, :, None])
        probs = weights / total[:, :, None]
        grad_probs = jnp.einsum(
            "thc,uc->htu", grad_three, bundle[2], preferred_element_type=jnp.float32
        )
        grad_scores = (
            probs * (grad_probs - jnp.transpose(delta)[:, :, None]) * score_scale
        ).astype(jnp.bfloat16)
        key_hat = dequantize(bundle[0], bundle[1])
        query_sum = query_sum + jnp.einsum(
            "htu,uc->thc", grad_scores, key_hat, preferred_element_type=jnp.float32
        )
        key_part = jnp.einsum(
            "htu,thc->uc", grad_scores, query_hat, preferred_element_type=jnp.float32
        )
        value_part = jnp.einsum(
            "htu,thc->uc",
            probs.astype(jnp.bfloat16),
            grad_three,
            preferred_element_type=jnp.float32,
        )
        if position == 0:
            own_part = (key_part, value_part)
        else:
            partials.append((key_part, value_part))
    key_back, value_back = return_grads(partials)
    attention_out = attended.reshape(tokens_dev, heads_count * head_size)
    query_grad = query_sum.astype(jnp.bfloat16).reshape(tokens_dev, heads_count * head_size)
    key_grad = (own_part[0] + key_back).astype(jnp.bfloat16)
    value_grad = (own_part[1] + value_back).astype(jnp.bfloat16)
    return (attention_out, query_grad, key_grad, value_grad)


def solution(mesh):
    return jax.shard_map(
        local,
        mesh=mesh,
        in_specs=(
            P(("row", "col"), None),
            P(("row", "col"), None),
            P(("row", "col"), None),
            P(("row", "col"), None),
            P(("row", "col"), None),
        ),
        out_specs=(
            P(("row", "col"), None),
            P(("row", "col"), None),
            P(("row", "col"), None),
            P(("row", "col"), None),
        ),
        check_vma=False,
    )
```

profile of v0, /device:TPU:30, one launch (start us, length us, event | category | flops | bytes accessed | tf_op | source)
XLA Modules:
  0.0 167.4 jit_solution(1891102752770029629)
XLA Ops:
  4.0 2.8 %collective-permute-start.2 = (bf16[512,128]{1,0:T(8,128)(2,1)S(1)}, bf16[512,128]{1,0:T(8,128)(2,1)S(1)}, u32[]{:S(2)}, u32[]{:S(2)}) collective-permute-start(bf16[512,128]{1,0:T(8,128)(2,1)S(1)} %fusion.69), channel_id=1, source_target_pairs={{0,2},{1,3},{2,4},{3,5},{4,6},{5,7},{6,8},{7,9},{8,10},{9,11},{10,... | collective-permute-start | bytes 393224 | tf_op jit(solution)/shard_map/ppermute | solution.py:14
  6.8 3.8 %collective-permute-start.8 = (bf16[512,128]{1,0:T(8,128)(2,1)S(1)}, bf16[512,128]{1,0:T(8,128)(2,1)S(1)}, u32[]{:S(2)}, u32[]{:S(2)}) collective-permute-start(bf16[512,128]{1,0:T(8,128)(2,1)S(1)} %fusion.69), channel_id=1, source_target_pairs={{0,16},{1,17},{2,18},{3,19},{4,20},{5,21},{6,22},{7,23},{8,24},{9,... | collective-permute-start | bytes 393224 | tf_op jit(solution)/shard_map/ppermute | solution.py:14
  10.7 3.7 %collective-permute-start.6 = (bf16[512,128]{1,0:T(8,128)(2,1)S(1)}, bf16[512,128]{1,0:T(8,128)(2,1)S(1)}, u32[]{:S(2)}, u32[]{:S(2)}) collective-permute-start(bf16[512,128]{1,0:T(8,128)(2,1)S(1)} %fusion.69), channel_id=1, source_target_pairs={{0,8},{1,9},{2,10},{3,11},{4,12},{5,13},{6,14},{7,15},{8,16},{9,17... | collective-permute-start | bytes 393224 | tf_op jit(solution)/shard_map/ppermute | solution.py:14
  14.3 3.6 %collective-permute-start.4 = (bf16[512,128]{1,0:T(8,128)(2,1)S(1)}, bf16[512,128]{1,0:T(8,128)(2,1)S(1)}, u32[]{:S(2)}, u32[]{:S(2)}) collective-permute-start(bf16[512,128]{1,0:T(8,128)(2,1)S(1)} %fusion.69), channel_id=1, source_target_pairs={{0,4},{1,5},{2,6},{3,7},{4,8},{5,9},{6,10},{7,11},{8,12},{9,13},{1... | collective-permute-start | bytes 393224 | tf_op jit(solution)/shard_map/ppermute | solution.py:14
  17.9 3.8 %collective-permute-start.1 = (bf16[512]{0:T(512)(128)(2,1)}, bf16[512]{0:T(512)(128)(2,1)}, u32[]{:S(2)}, u32[]{:S(2)}) collective-permute-start(bf16[512]{0:T(512)(128)(2,1)} %get-tuple-element.32), channel_id=1, source_target_pairs={{0,1},{1,2},{2,3},{3,4},{4,5},{5,6},{6,7},{7,8},{8,9},{9,10},{10,1... | collective-permute-start | bytes 3080 | tf_op jit(solution)/shard_map/ppermute | solution.py:14
  31.0 2.0 %collective-permute-start.3 = (bf16[512]{0:T(512)(128)(2,1)}, bf16[512]{0:T(512)(128)(2,1)S(1)}, u32[]{:S(2)}, u32[]{:S(2)}) collective-permute-start(bf16[512]{0:T(512)(128)(2,1)} %get-tuple-element.32), channel_id=1, source_target_pairs={{0,2},{1,3},{2,4},{3,5},{4,6},{5,7},{6,8},{7,9},{8,10},{9,11},{10,... | collective-permute-start | bytes 3080 | tf_op jit(solution)/shard_map/ppermute | solution.py:14
  33.7 4.5 %collective-permute-done.3 = bf16[512]{0:T(512)(128)(2,1)S(1)} collective-permute-done((bf16[512]{0:T(512)(128)(2,1)}, bf16[512]{0:T(512)(128)(2,1)S(1)}, u32[]{:S(2)}, u32[]{:S(2)}) %collective-permute-start.3) | collective-permute-done | bytes 1056 | tf_op jit(solution)/shard_map/ppermute | solution.py:14
  38.2 1.9 %collective-permute-start.5 = (bf16[512]{0:T(512)(128)(2,1)}, bf16[512]{0:T(512)(128)(2,1)S(1)}, u32[]{:S(2)}, u32[]{:S(2)}) collective-permute-start(bf16[512]{0:T(512)(128)(2,1)} %get-tuple-element.32), channel_id=1, source_target_pairs={{0,4},{1,5},{2,6},{3,7},{4,8},{5,9},{6,10},{7,11},{8,12},{9,13},{1... | collective-permute-start | bytes 3080 | tf_op jit(solution)/shard_map/ppermute | solution.py:14
  40.1 3.7 %collective-permute-done.5 = bf16[512]{0:T(512)(128)(2,1)S(1)} collective-permute-done((bf16[512]{0:T(512)(128)(2,1)}, bf16[512]{0:T(512)(128)(2,1)S(1)}, u32[]{:S(2)}, u32[]{:S(2)}) %collective-permute-start.5) | collective-permute-done | bytes 1056 | tf_op jit(solution)/shard_map/ppermute | solution.py:14
  45.8 6.8 %collective-permute-done.7 = bf16[512]{0:T(512)(128)(2,1)S(1)} collective-permute-done((bf16[512]{0:T(512)(128)(2,1)}, bf16[512]{0:T(512)(128)(2,1)S(1)}, u32[]{:S(2)}, u32[]{:S(2)}) %collective-permute-start.7) | collective-permute-done | bytes 1056 | tf_op jit(solution)/shard_map/ppermute | solution.py:14
  55.2 6.7 %collective-permute-done.9 = bf16[512]{0:T(512)(128)(2,1)S(1)} collective-permute-done((bf16[512]{0:T(512)(128)(2,1)}, bf16[512]{0:T(512)(128)(2,1)S(1)}, u32[]{:S(2)}, u32[]{:S(2)}) %collective-permute-start.9) | collective-permute-done | bytes 1056 | tf_op jit(solution)/shard_map/ppermute | solution.py:14
  61.8 1.9 %collective-permute-start = (bf16[512,128]{1,0:T(8,128)(2,1)S(1)}, bf16[512,128]{1,0:T(8,128)(2,1)S(1)}, u32[]{:S(2)}, u32[]{:S(2)}) collective-permute-start(bf16[512,128]{1,0:T(8,128)(2,1)S(1)} %fusion.69), channel_id=1, source_target_pairs={{0,1},{1,2},{2,3},{3,4},{4,5},{5,6},{6,7},{7,8},{8,9},{9,10},{10,1... | collective-permute-start | bytes 393224 | tf_op jit(solution)/shard_map/ppermute | solution.py:14
  63.8 1.9 %collective-permute-start.10 = (bf16[512,128]{0,1:T(8,128)(2,1)S(1)}, bf16[512,128]{0,1:T(8,128)(2,1)S(1)}, u32[]{:S(2)}, u32[]{:S(2)}) collective-permute-start(bf16[512,128]{0,1:T(8,128)(2,1)S(1)} %copy.163), channel_id=1, source_target_pairs={{0,1},{1,2},{2,3},{3,4},{4,5},{5,6},{6,7},{7,8},{8,9},{9,10},{10,1... | collective-permute-start | bytes 393224 | tf_op jit(solution)/shard_map/ppermute | solution.py:14
  66.2 1.9 %collective-permute-start.12 = (bf16[512,128]{0,1:T(8,128)(2,1)S(1)}, bf16[512,128]{0,1:T(8,128)(2,1)S(1)}, u32[]{:S(2)}, u32[]{:S(2)}) collective-permute-start(bf16[512,128]{0,1:T(8,128)(2,1)S(1)} %copy.163), channel_id=1, source_target_pairs={{0,4},{1,5},{2,6},{3,7},{4,8},{5,9},{6,10},{7,11},{8,12},{9,13},{1... | collective-permute-start | bytes 393224 | tf_op jit(solution)/shard_map/ppermute | solution.py:14
  68.6 2.2 %collective-permute-start.13 = (bf16[512,128]{0,1:T(8,128)(2,1)S(1)}, bf16[512,128]{0,1:T(8,128)(2,1)S(1)}, u32[]{:S(2)}, u32[]{:S(2)}) collective-permute-start(bf16[512,128]{0,1:T(8,128)(2,1)S(1)} %copy.163), channel_id=1, source_target_pairs={{0,8},{1,9},{2,10},{3,11},{4,12},{5,13},{6,14},{7,15},{8,16},{9,17... | collective-permute-start | bytes 393224 | tf_op jit(solution)/shard_map/ppermute | solution.py:14
  71.2 1.9 %collective-permute-start.14 = (bf16[512,128]{0,1:T(8,128)(2,1)S(1)}, bf16[512,128]{0,1:T(8,128)(2,1)S(1)}, u32[]{:S(2)}, u32[]{:S(2)}) collective-permute-start(bf16[512,128]{0,1:T(8,128)(2,1)S(1)} %copy.163), channel_id=1, source_target_pairs={{0,16},{1,17},{2,18},{3,19},{4,20},{5,21},{6,22},{7,23},{8,24},{9,... | collective-permute-start | bytes 393224 | tf_op jit(solution)/shard_map/ppermute | solution.py:14
  73.6 4.6 %collective-permute-start.11 = (bf16[512,128]{0,1:T(8,128)(2,1)S(1)}, bf16[512,128]{0,1:T(8,128)(2,1)S(1)}, u32[]{:S(2)}, u32[]{:S(2)}) collective-permute-start(bf16[512,128]{0,1:T(8,128)(2,1)S(1)} %copy.163), channel_id=1, source_target_pairs={{0,2},{1,3},{2,4},{3,5},{4,6},{5,7},{6,8},{7,9},{8,10},{9,11},{10,... | collective-permute-start | bytes 393224 | tf_op jit(solution)/shard_map/ppermute | solution.py:14
  78.2 2.1 %fusion.31 = (f32[2,512]{1,0:T(2,128)S(1)}, f32[2,512]{1,0:T(2,128)S(1)}, f32[2,512]{1,0:T(2,128)S(1)}, f32[2,512]{1,0:T(2,128)S(1)}, f32[2,512]{1,0:T(2,128)S(1...) fusion(f32[512]{0:T(512)S(1)} %convert_element_type.236, f32[2,512]{1,0:T(2,128)S(1)} %get-tuple-element.34, ...), kind=kOutput, calls=%fused_computation.49 | convolution fusion | flops 146794496 | bytes 13279237 | tf_op jit(solution)/shard_map/thc,uc->htu/dot_general | solution.py:34
  80.9 2.8 %fusion.114 = (f32[2,512]{1,0:T(2,128)S(1)}, f32[2,512]{1,0:T(2,128)S(1)}, f32[2,512]{1,0:T(2,128)S(1)}, f32[2,512]{1,0:T(2,128)S(1)}, f32[2,512]{1,0:T(2,128)S(1)}) fusion(f32[2,512]{1,0:T(2,128)S(1)} %maximum_maximum_fusion, f32[512]{0:T(512)S(1)} %convert_element_type.236, f32[2,512]{1,0:T(2,128)S(1)} %get-tuple-element.34, ...), kind=kLoop, calls=%fused_computation.175 | loop fusion | flops 13102080 | bytes 10786820 | tf_op jit(solution)/shard_map/reduce_sum | solution.py:89
  91.7 3.2 %collective-permute-start.21 = (f32[512,128]{1,0:T(8,128)}, f32[512,128]{1,0:T(8,128)}, u32[]{:S(2)}, u32[]{:S(2)}) collective-permute-start(f32[512,128]{1,0:T(8,128)} %convolution_bitcast_fusion.3), channel_id=1, source_target_pairs={{2,0},{3,1},{4,2},{5,3},{6,4},{7,5},{8,6},{9,7},{10,8},{11,9},{12,... | collective-permute-start | bytes 786440 | tf_op jit(solution)/shard_map/ppermute | solution.py:14
  95.7 3.4 %collective-permute-start.20 = (f32[512,128]{1,0:T(8,128)}, f32[512,128]{1,0:T(8,128)}, u32[]{:S(2)}, u32[]{:S(2)}) collective-permute-start(f32[512,128]{1,0:T(8,128)} %convolution_bitcast_fusion.4), channel_id=1, source_target_pairs={{1,0},{2,1},{3,2},{4,3},{5,4},{6,5},{7,6},{8,7},{9,8},{10,9},{11,1... | collective-permute-start | bytes 786440 | tf_op jit(solution)/shard_map/ppermute | solution.py:14
  99.8 4.6 %collective-permute-start.22 = (f32[512,128]{1,0:T(8,128)}, f32[512,128]{1,0:T(8,128)}, u32[]{:S(2)}, u32[]{:S(2)}) collective-permute-start(f32[512,128]{1,0:T(8,128)} %convolution_bitcast_fusion.2), channel_id=1, source_target_pairs={{4,0},{5,1},{6,2},{7,3},{8,4},{9,5},{10,6},{11,7},{12,8},{13,9},{1... | collective-permute-start | bytes 786440 | tf_op jit(solution)/shard_map/ppermute | solution.py:14
  105.1 6.8 %collective-permute-start.23 = (f32[512,128]{1,0:T(8,128)}, f32[512,128]{1,0:T(8,128)}, u32[]{:S(2)}, u32[]{:S(2)}) collective-permute-start(f32[512,128]{1,0:T(8,128)} %convolution_bitcast_fusion.1), channel_id=1, source_target_pairs={{8,0},{9,1},{10,2},{11,3},{12,4},{13,5},{14,6},{15,7},{16,8},{17,9... | collective-permute-start | bytes 786440 | tf_op jit(solution)/shard_map/ppermute | solution.py:14
  112.6 3.9 %collective-permute-start.24 = (f32[512,128]{1,0:T(8,128)}, f32[512,128]{1,0:T(8,128)}, u32[]{:S(2)}, u32[]{:S(2)}) collective-permute-start(f32[512,128]{1,0:T(8,128)} %convolution_bitcast_fusion), channel_id=1, source_target_pairs={{16,0},{17,1},{18,2},{19,3},{20,4},{21,5},{22,6},{23,7},{24,8},{25... | collective-permute-start | bytes 786440 | tf_op jit(solution)/shard_map/ppermute | solution.py:14
  136.6 3.8 %collective-permute-start.19 = (f32[512,128]{1,0:T(8,128)}, f32[512,128]{1,0:T(8,128)S(1)}, u32[]{:S(2)}, u32[]{:S(2)}) collective-permute-start(f32[512,128]{1,0:T(8,128)} %convolution_bitcast_fusion.6), channel_id=1, source_target_pairs={{16,0},{17,1},{18,2},{19,3},{20,4},{21,5},{22,6},{23,7},{24,8},{25... | collective-permute-start | bytes 786440 | tf_op jit(solution)/shard_map/ppermute | solution.py:14
  140.5 1.9 %collective-permute-start.18 = (f32[512,128]{1,0:T(8,128)}, f32[512,128]{1,0:T(8,128)S(1)}, u32[]{:S(2)}, u32[]{:S(2)}) collective-permute-start(f32[512,128]{1,0:T(8,128)} %convolution_bitcast_fusion.7), channel_id=1, source_target_pairs={{8,0},{9,1},{10,2},{11,3},{12,4},{13,5},{14,6},{15,7},{16,8},{17,9... | collective-permute-start | bytes 786440 | tf_op jit(solution)/shard_map/ppermute | solution.py:14
  142.4 1.9 %collective-permute-start.17 = (f32[512,128]{1,0:T(8,128)}, f32[512,128]{1,0:T(8,128)S(1)}, u32[]{:S(2)}, u32[]{:S(2)}) collective-permute-start(f32[512,128]{1,0:T(8,128)} %convolution_bitcast_fusion.8), channel_id=1, source_target_pairs={{4,0},{5,1},{6,2},{7,3},{8,4},{9,5},{10,6},{11,7},{12,8},{13,9},{1... | collective-permute-start | bytes 786440 | tf_op jit(solution)/shard_map/ppermute | solution.py:14
  144.3 3.9 %collective-permute-start.16 = (f32[512,128]{1,0:T(8,128)}, f32[512,128]{1,0:T(8,128)S(1)}, u32[]{:S(2)}, u32[]{:S(2)}) collective-permute-start(f32[512,128]{1,0:T(8,128)} %convolution_bitcast_fusion.9), channel_id=1, source_target_pairs={{2,0},{3,1},{4,2},{5,3},{6,4},{7,5},{8,6},{9,7},{10,8},{11,9},{12,... | collective-permute-start | bytes 786440 | tf_op jit(solution)/shard_map/ppermute | solution.py:14
  148.3 3.9 %collective-permute-start.15 = (f32[512,128]{1,0:T(8,128)S(1)}, f32[512,128]{1,0:T(8,128)S(1)}, u32[]{:S(2)}, u32[]{:S(2)}) collective-permute-start(f32[512,128]{1,0:T(8,128)S(1)} %convolution_bitcast_fusion.10), channel_id=1, source_target_pairs={{1,0},{2,1},{3,2},{4,3},{5,4},{6,5},{7,6},{8,7},{9,8},{10,9},{11,1... | collective-permute-start | bytes 786440 | tf_op jit(solution)/shard_map/ppermute | solution.py:14
  152.2 3.0 %fusion.62 = bf16[512,128]{1,0:T(8,128)(2,1)} fusion(bf16[512,2,128]{0,2,1:T(8,128)(2,1)} %bitcast.332, f32[2,512]{1,0:T(2,128)S(1)} %copy-done.18, f32[512,128]{1,0:T(8,128)} %collective-permute-done.24, f32[512,128]{1,0:T(8,128)} %collective-permute-done.23, f32[512,128]{1,0:T(8,128)} %collective-permute-done.22, ...), kind=kOutput, calls=%fused_computation.104 | convolution fusion | flops 137756672 | bytes 4077568 | tf_op jit(solution)/shard_map/htu,thc->uc/dot_general | solution.py:117
  155.1 7.3 %collective-permute-done.16 = f32[512,128]{1,0:T(8,128)S(1)} collective-permute-done((f32[512,128]{1,0:T(8,128)}, f32[512,128]{1,0:T(8,128)S(1)}, u32[]{:S(2)}, u32[]{:S(2)}) %collective-permute-start.16) | collective-permute-done | bytes 262176 | tf_op jit(solution)/shard_map/ppermute | solution.py:14
  162.4 3.7 %collective-permute-done.15 = f32[512,128]{1,0:T(8,128)S(1)} collective-permute-done((f32[512,128]{1,0:T(8,128)S(1)}, f32[512,128]{1,0:T(8,128)S(1)}, u32[]{:S(2)}, u32[]{:S(2)}) %collective-permute-start.15) | collective-permute-done | bytes 262176 | tf_op jit(solution)/shard_map/ppermute | solution.py:14
  (122 shorter events, 48.8 us)
Async XLA Ops:
  4.0 59.8 %collective-permute-start.2 = (bf16[512,128]{1,0:T(8,128)(2,1)S(1)}, bf16[512,128]{1,0:T(8,128)(2,1)S(1)}, u32[]{:S(2)}, u32[]{:S(2)}) collective-permute-start(bf16[512,128]{1,0:T(8,128)(2,1)S(1)} %fusion.69), channel_id=1, source_target_pairs={{0,2},{1,3},{2,4},{3,5},{4,6},{5,7},{6,8},{7,9},{8,10},{9,11},{10,... | collective-permute-start | bytes 393224 | tf_op jit(solution)/shard_map/ppermute | solution.py:14
  6.8 59.3 %collective-permute-start.8 = (bf16[512,128]{1,0:T(8,128)(2,1)S(1)}, bf16[512,128]{1,0:T(8,128)(2,1)S(1)}, u32[]{:S(2)}, u32[]{:S(2)}) collective-permute-start(bf16[512,128]{1,0:T(8,128)(2,1)S(1)} %fusion.69), channel_id=1, source_target_pairs={{0,16},{1,17},{2,18},{3,19},{4,20},{5,21},{6,22},{7,23},{8,24},{9,... | collective-permute-start | bytes 393224 | tf_op jit(solution)/shard_map/ppermute | solution.py:14
  10.7 57.9 %collective-permute-start.6 = (bf16[512,128]{1,0:T(8,128)(2,1)S(1)}, bf16[512,128]{1,0:T(8,128)(2,1)S(1)}, u32[]{:S(2)}, u32[]{:S(2)}) collective-permute-start(bf16[512,128]{1,0:T(8,128)(2,1)S(1)} %fusion.69), channel_id=1, source_target_pairs={{0,8},{1,9},{2,10},{3,11},{4,12},{5,13},{6,14},{7,15},{8,16},{9,17... | collective-permute-start | bytes 393224 | tf_op jit(solution)/shard_map/ppermute | solution.py:14
  14.3 56.9 %collective-permute-start.4 = (bf16[512,128]{1,0:T(8,128)(2,1)S(1)}, bf16[512,128]{1,0:T(8,128)(2,1)S(1)}, u32[]{:S(2)}, u32[]{:S(2)}) collective-permute-start(bf16[512,128]{1,0:T(8,128)(2,1)S(1)} %fusion.69), channel_id=1, source_target_pairs={{0,4},{1,5},{2,6},{3,7},{4,8},{5,9},{6,10},{7,11},{8,12},{9,13},{1... | collective-permute-start | bytes 393224 | tf_op jit(solution)/shard_map/ppermute | solution.py:14
  17.9 13.1 %collective-permute-start.1 = (bf16[512]{0:T(512)(128)(2,1)}, bf16[512]{0:T(512)(128)(2,1)}, u32[]{:S(2)}, u32[]{:S(2)}) collective-permute-start(bf16[512]{0:T(512)(128)(2,1)} %get-tuple-element.32), channel_id=1, source_target_pairs={{0,1},{1,2},{2,3},{3,4},{4,5},{5,6},{6,7},{7,8},{8,9},{9,10},{10,1... | collective-permute-start | bytes 3080 | tf_op jit(solution)/shard_map/ppermute | solution.py:14
  23.1 94.9 %copy-start.2 = (pred[512,512]{0,1:T(8,128)(4,1)}, pred[512,512]{0,1:T(8,128)(4,1)S(1)}, u32[]{:S(2)}) copy-start(pred[512,512]{0,1:T(8,128)(4,1)S(1)} %iota_compare_fusion) | copy-start | bytes 786436
  31.0 7.2 %collective-permute-start.3 = (bf16[512]{0:T(512)(128)(2,1)}, bf16[512]{0:T(512)(128)(2,1)S(1)}, u32[]{:S(2)}, u32[]{:S(2)}) collective-permute-start(bf16[512]{0:T(512)(128)(2,1)} %get-tuple-element.32), channel_id=1, source_target_pairs={{0,2},{1,3},{2,4},{3,5},{4,6},{5,7},{6,8},{7,9},{8,10},{9,11},{10,... | collective-permute-start | bytes 3080 | tf_op jit(solution)/shard_map/ppermute | solution.py:14
  38.2 5.7 %collective-permute-start.5 = (bf16[512]{0:T(512)(128)(2,1)}, bf16[512]{0:T(512)(128)(2,1)S(1)}, u32[]{:S(2)}, u32[]{:S(2)}) collective-permute-start(bf16[512]{0:T(512)(128)(2,1)} %get-tuple-element.32), channel_id=1, source_target_pairs={{0,4},{1,5},{2,6},{3,7},{4,8},{5,9},{6,10},{7,11},{8,12},{9,13},{1... | collective-permute-start | bytes 3080 | tf_op jit(solution)/shard_map/ppermute | solution.py:14
  43.8 8.7 %collective-permute-start.7 = (bf16[512]{0:T(512)(128)(2,1)}, bf16[512]{0:T(512)(128)(2,1)S(1)}, u32[]{:S(2)}, u32[]{:S(2)}) collective-permute-start(bf16[512]{0:T(512)(128)(2,1)} %get-tuple-element.32), channel_id=1, source_target_pairs={{0,8},{1,9},{2,10},{3,11},{4,12},{5,13},{6,14},{7,15},{8,16},{9,17... | collective-permute-start | bytes 3080 | tf_op jit(solution)/shard_map/ppermute | solution.py:14
  52.5 9.3 %collective-permute-start.9 = (bf16[512]{0:T(512)(128)(2,1)}, bf16[512]{0:T(512)(128)(2,1)S(1)}, u32[]{:S(2)}, u32[]{:S(2)}) collective-permute-start(bf16[512]{0:T(512)(128)(2,1)} %get-tuple-element.32), channel_id=1, source_target_pairs={{0,16},{1,17},{2,18},{3,19},{4,20},{5,21},{6,22},{7,23},{8,24},{9,... | collective-permute-start | bytes 3080 | tf_op jit(solution)/shard_map/ppermute | solution.py:14
  61.8 11.8 %collective-permute-start = (bf16[512,128]{1,0:T(8,128)(2,1)S(1)}, bf16[512,128]{1,0:T(8,128)(2,1)S(1)}, u32[]{:S(2)}, u32[]{:S(2)}) collective-permute-start(bf16[512,128]{1,0:T(8,128)(2,1)S(1)} %fusion.69), channel_id=1, source_target_pairs={{0,1},{1,2},{2,3},{3,4},{4,5},{5,6},{6,7},{7,8},{8,9},{9,10},{10,1... | collective-permute-start | bytes 393224 | tf_op jit(solution)/shard_map/ppermute | solution.py:14
  63.8 27.9 %collective-permute-start.10 = (bf16[512,128]{0,1:T(8,128)(2,1)S(1)}, bf16[512,128]{0,1:T(8,128)(2,1)S(1)}, u32[]{:S(2)}, u32[]{:S(2)}) collective-permute-start(bf16[512,128]{0,1:T(8,128)(2,1)S(1)} %copy.163), channel_id=1, source_target_pairs={{0,1},{1,2},{2,3},{3,4},{4,5},{5,6},{6,7},{7,8},{8,9},{9,10},{10,1... | collective-permute-start | bytes 393224 | tf_op jit(solution)/shard_map/ppermute | solution.py:14
  66.2 29.5 %collective-permute-start.12 = (bf16[512,128]{0,1:T(8,128)(2,1)S(1)}, bf16[512,128]{0,1:T(8,128)(2,1)S(1)}, u32[]{:S(2)}, u32[]{:S(2)}) collective-permute-start(bf16[512,128]{0,1:T(8,128)(2,1)S(1)} %copy.163), channel_id=1, source_target_pairs={{0,4},{1,5},{2,6},{3,7},{4,8},{5,9},{6,10},{7,11},{8,12},{9,13},{1... | collective-permute-start | bytes 393224 | tf_op jit(solution)/shard_map/ppermute | solution.py:14
  68.5 9.7 %copy-start.15 = (f32[512]{0:T(512)S(1)}, f32[512]{0:T(512)}, u32[]{:S(2)}) copy-start(f32[512]{0:T(512)} %convert_element_type.231) | copy-start | bytes 6148
  68.6 31.2 %collective-permute-start.13 = (bf16[512,128]{0,1:T(8,128)(2,1)S(1)}, bf16[512,128]{0,1:T(8,128)(2,1)S(1)}, u32[]{:S(2)}, u32[]{:S(2)}) collective-permute-start(bf16[512,128]{0,1:T(8,128)(2,1)S(1)} %copy.163), channel_id=1, source_target_pairs={{0,8},{1,9},{2,10},{3,11},{4,12},{5,13},{6,14},{7,15},{8,16},{9,17... | collective-permute-start | bytes 393224 | tf_op jit(solution)/shard_map/ppermute | solution.py:14
  71.2 9.1 %copy-start.9 = (bf16[512,128]{1,0:T(8,128)(2,1)}, bf16[512,128]{1,0:T(8,128)(2,1)S(1)}, u32[]{:S(2)}) copy-start(bf16[512,128]{1,0:T(8,128)(2,1)S(1)} %collective-permute-done.4) | copy-start | bytes 393220
  71.2 33.9 %collective-permute-start.14 = (bf16[512,128]{0,1:T(8,128)(2,1)S(1)}, bf16[512,128]{0,1:T(8,128)(2,1)S(1)}, u32[]{:S(2)}, u32[]{:S(2)}) collective-permute-start(bf16[512,128]{0,1:T(8,128)(2,1)S(1)} %copy.163), channel_id=1, source_target_pairs={{0,16},{1,17},{2,18},{3,19},{4,20},{5,21},{6,22},{7,23},{8,24},{9,... | collective-permute-start | bytes 393224 | tf_op jit(solution)/shard_map/ppermute | solution.py:14
  73.6 39.0 %collective-permute-start.11 = (bf16[512,128]{0,1:T(8,128)(2,1)S(1)}, bf16[512,128]{0,1:T(8,128)(2,1)S(1)}, u32[]{:S(2)}, u32[]{:S(2)}) collective-permute-start(bf16[512,128]{0,1:T(8,128)(2,1)S(1)} %copy.163), channel_id=1, source_target_pairs={{0,2},{1,3},{2,4},{3,5},{4,6},{5,7},{6,8},{7,9},{8,10},{9,11},{10,... | collective-permute-start | bytes 393224 | tf_op jit(solution)/shard_map/ppermute | solution.py:14
  83.7 43.0 %copy-start.17 = (f32[2,512]{1,0:T(2,128)}, f32[2,512]{1,0:T(2,128)S(1)}, u32[]{:S(2)}) copy-start(f32[2,512]{1,0:T(2,128)S(1)} %add_add_fusion) | copy-start | bytes 12292
  91.7 44.9 %collective-permute-start.21 = (f32[512,128]{1,0:T(8,128)}, f32[512,128]{1,0:T(8,128)}, u32[]{:S(2)}, u32[]{:S(2)}) collective-permute-start(f32[512,128]{1,0:T(8,128)} %convolution_bitcast_fusion.3), channel_id=1, source_target_pairs={{2,0},{3,1},{4,2},{5,3},{6,4},{7,5},{8,6},{9,7},{10,8},{11,9},{12,... | collective-permute-start | bytes 786440 | tf_op jit(solution)/shard_map/ppermute | solution.py:14
  95.7 44.8 %collective-permute-start.20 = (f32[512,128]{1,0:T(8,128)}, f32[512,128]{1,0:T(8,128)}, u32[]{:S(2)}, u32[]{:S(2)}) collective-permute-start(f32[512,128]{1,0:T(8,128)} %convolution_bitcast_fusion.4), channel_id=1, source_target_pairs={{1,0},{2,1},{3,2},{4,3},{5,4},{6,5},{7,6},{8,7},{9,8},{10,9},{11,1... | collective-permute-start | bytes 786440 | tf_op jit(solution)/shard_map/ppermute | solution.py:14
  99.8 42.6 %collective-permute-start.22 = (f32[512,128]{1,0:T(8,128)}, f32[512,128]{1,0:T(8,128)}, u32[]{:S(2)}, u32[]{:S(2)}) collective-permute-start(f32[512,128]{1,0:T(8,128)} %convolution_bitcast_fusion.2), channel_id=1, source_target_pairs={{4,0},{5,1},{6,2},{7,3},{8,4},{9,5},{10,6},{11,7},{12,8},{13,9},{1... | collective-permute-start | bytes 786440 | tf_op jit(solution)/shard_map/ppermute | solution.py:14
  105.1 39.2 %collective-permute-start.23 = (f32[512,128]{1,0:T(8,128)}, f32[512,128]{1,0:T(8,128)}, u32[]{:S(2)}, u32[]{:S(2)}) collective-permute-start(f32[512,128]{1,0:T(8,128)} %convolution_bitcast_fusion.1), channel_id=1, source_target_pairs={{8,0},{9,1},{10,2},{11,3},{12,4},{13,5},{14,6},{15,7},{16,8},{17,9... | collective-permute-start | bytes 786440 | tf_op jit(solution)/shard_map/ppermute | solution.py:14
  112.6 35.6 %collective-permute-start.24 = (f32[512,128]{1,0:T(8,128)}, f32[512,128]{1,0:T(8,128)}, u32[]{:S(2)}, u32[]{:S(2)}) collective-permute-start(f32[512,128]{1,0:T(8,128)} %convolution_bitcast_fusion), channel_id=1, source_target_pairs={{16,0},{17,1},{18,2},{19,3},{20,4},{21,5},{22,6},{23,7},{24,8},{25... | collective-permute-start | bytes 786440 | tf_op jit(solution)/shard_map/ppermute | solution.py:14
  119.0 6.4 %copy-start = (bf16[2,512,512]{1,2,0:T(8,128)(2,1)}, bf16[2,512,512]{1,2,0:T(8,128)(2,1)S(1)}, u32[]{:S(2)}) copy-start(bf16[2,512,512]{1,2,0:T(8,128)(2,1)S(1)} %fusion.17) | copy-start | bytes 3145732
  131.2 20.9 %copy-start.18 = (f32[2,512]{1,0:T(2,128)S(1)}, f32[2,512]{1,0:T(2,128)}, u32[]{:S(2)}) copy-start(f32[2,512]{1,0:T(2,128)} %copy-done.17) | copy-start | bytes 12292
  136.6 29.6 %copy-start.1 = (bf16[2,512,512]{1,2,0:T(8,128)(2,1)S(1)}, bf16[2,512,512]{1,2,0:T(8,128)(2,1)}, u32[]{:S(2)}) copy-start(bf16[2,512,512]{1,2,0:T(8,128)(2,1)} %copy-done) | copy-start | bytes 3145732
  136.6 18.5 %collective-permute-start.19 = (f32[512,128]{1,0:T(8,128)}, f32[512,128]{1,0:T(8,128)S(1)}, u32[]{:S(2)}, u32[]{:S(2)}) collective-permute-start(f32[512,128]{1,0:T(8,128)} %convolution_bitcast_fusion.6), channel_id=1, source_target_pairs={{16,0},{17,1},{18,2},{19,3},{20,4},{21,5},{22,6},{23,7},{24,8},{25... | collective-permute-start | bytes 786440 | tf_op jit(solution)/shard_map/ppermute | solution.py:14
  140.5 14.7 %collective-permute-start.18 = (f32[512,128]{1,0:T(8,128)}, f32[512,128]{1,0:T(8,128)S(1)}, u32[]{:S(2)}, u32[]{:S(2)}) collective-permute-start(f32[512,128]{1,0:T(8,128)} %convolution_bitcast_fusion.7), channel_id=1, source_target_pairs={{8,0},{9,1},{10,2},{11,3},{12,4},{13,5},{14,6},{15,7},{16,8},{17,9... | collective-permute-start | bytes 786440 | tf_op jit(solution)/shard_map/ppermute | solution.py:14
  142.4 12.7 %collective-permute-start.17 = (f32[512,128]{1,0:T(8,128)}, f32[512,128]{1,0:T(8,128)S(1)}, u32[]{:S(2)}, u32[]{:S(2)}) collective-permute-start(f32[512,128]{1,0:T(8,128)} %convolution_bitcast_fusion.8), channel_id=1, source_target_pairs={{4,0},{5,1},{6,2},{7,3},{8,4},{9,5},{10,6},{11,7},{12,8},{13,9},{1... | collective-permute-start | bytes 786440 | tf_op jit(solution)/shard_map/ppermute | solution.py:14
  144.3 18.1 %collective-permute-start.16 = (f32[512,128]{1,0:T(8,128)}, f32[512,128]{1,0:T(8,128)S(1)}, u32[]{:S(2)}, u32[]{:S(2)}) collective-permute-start(f32[512,128]{1,0:T(8,128)} %convolution_bitcast_fusion.9), channel_id=1, source_target_pairs={{2,0},{3,1},{4,2},{5,3},{6,4},{7,5},{8,6},{9,7},{10,8},{11,9},{12,... | collective-permute-start | bytes 786440 | tf_op jit(solution)/shard_map/ppermute | solution.py:14
  148.3 17.9 %collective-permute-start.15 = (f32[512,128]{1,0:T(8,128)S(1)}, f32[512,128]{1,0:T(8,128)S(1)}, u32[]{:S(2)}, u32[]{:S(2)}) collective-permute-start(f32[512,128]{1,0:T(8,128)S(1)} %convolution_bitcast_fusion.10), channel_id=1, source_target_pairs={{1,0},{2,1},{3,2},{4,3},{5,4},{6,5},{7,6},{8,7},{9,8},{10,9},{11,1... | collective-permute-start | bytes 786440 | tf_op jit(solution)/shard_map/ppermute | solution.py:14
  (12 other events, 31.2 us)
where the time goes:
time: 169 us; the launch traced here: 167 us
  starting transfers between devices  77.2 us (46%)
  matrix products  35.1 us (21%)
  waiting for transfers between devices  32.7 us (19%)
  other arithmetic  9.78 us (6%)
  local copies, waits for them, and re-layouts  7.89 us (5%)
  between operations  4.76 us (3%)
    ppermute x25, starting transfers between devices, shifted(): lax.ppermute(value, axis, [(source, source + steps) for source in range(l...  77.2 us
    ppermute x25, waiting for transfers between devices, shifted(): lax.ppermute(value, axis, [(source, source + steps) for source in range(l...  32.7 us
    dot_general x6, matrix products, local(): jnp.einsum('htu,thc->uc', probs.astype(jnp.bfloat16), grad_three, preferr...  10.1 us
    unnamed x43, local copies, waits for them, and re-layouts  7.12 us
    dot_general x6, matrix products, local(): jnp.einsum('htu,thc->uc', grad_scores, query_hat, preferred_element_type=...  6.76 us
    dot_general x6, matrix products, local(): jnp.einsum('thc,uc->htu', grad_three, bundle[2], preferred_element_type=j...  5.4 us
    dot_general x6, matrix products, local(): jnp.einsum('htu,uc->thc', weights.astype(jnp.bfloat16), bundle[2], prefer...  5.11 us
    dot_general x6, matrix products, score_block(): jnp.einsum('thc,uc->htu', query_codes, key_codes, preferred_element_type=...  4.22 us
  transfers between devices with their start and end apart: 25, of which 6 were waited for; matrix products, arithmetic and copies ran while one was open for 29% of the time, Pallas kernels for 0%

commit v1 on v0

v1 whole, which is shorter than its diff:
```python
import functools
import math

import jax
import jax.numpy as jnp
from jax import lax
from jax.experimental import pallas as pl
from jax.experimental.pallas import tpu as pltpu
from jax.sharding import PartitionSpec as P

scale_eps = 1e-06
MESH = pl.DeviceIdType.MESH
bf16 = jnp.bfloat16
f32 = jnp.float32


def quantize(values):
    largest = jnp.max(jnp.abs(values), axis=1, keepdims=True)
    scales = (largest + scale_eps).astype(bf16).astype(f32)
    codes = jnp.clip(jnp.floor(values * (127.0 / scales) + 0.5), -127.0, 127.0)
    return codes, scales


def dot(left, right):
    return jnp.dot(left, right, preferred_element_type=f32)


def kernel(
    rows, cols, levels, chunk,
    q_ref, k_ref, v_ref, g_ref, link_ref,
    out_ref, dq_ref, dk_ref, dv_ref,
    k_in, v_in, part_out, part_in,
    q_codes_t, q_hat, g_rows, g_aug_t, k_hat_t, v_aug, probs, mixed_t, dq_t, probs_now, ds_now,
    tops, sums, weight_ref,
    send_k, recv_k, send_v, recv_v, send_part, recv_part,
):
    tokens, head = k_ref.shape
    heads = q_ref.shape[1] // head
    width = heads * tokens
    blocks = rows * cols
    block_id = lax.axis_index("row") * cols + lax.axis_index("col")
    score_scale = 1.0 / math.sqrt(head)

    def place(block):
        return (block // cols, lax.rem(block, cols))

    def ahead(distance):
        return place(lax.rem(block_id + distance, blocks))

    def behind(distance):
        return place(lax.rem(block_id + (blocks - distance), blocks))

    barrier = pltpu.get_barrier_semaphore()
    for level in range(levels):
        for partner in (ahead(2**level), behind(2**level)):
            pl.semaphore_signal(barrier, inc=1, device_id=partner, device_id_type=MESH)
    pl.semaphore_wait(barrier, 2 * levels)

    sends = []
    for level in range(levels):
        for source, target, send, recv in (
            (k_ref, k_in, send_k, recv_k),
            (v_ref, v_in, send_v, recv_v),
        ):
            copy = pltpu.make_async_remote_copy(
                src_ref=source,
                dst_ref=target.at[level],
                send_sem=send.at[level],
                recv_sem=recv.at[level],
                device_id=ahead(2**level),
                device_id_type=MESH,
            )
            copy.start()
            sends.append(copy)

    row_factors = []
    for h in range(heads):
        span = pl.ds(h * tokens, tokens)
        codes, scales = quantize(q_ref[:, h * head : (h + 1) * head].astype(f32))
        q_hat[span, :] = (codes * (scales / 127.0)).astype(bf16)
        codes_t = jnp.transpose(codes).astype(bf16)
        q_codes_t[:head, span] = codes_t
        q_codes_t[head:, span] = codes_t
        factor = scales * (1.0 / (127.0 * 127.0 * math.sqrt(head))) * (1.0 / math.log(2.0))
        row_factors.append(jnp.transpose(jnp.broadcast_to(factor, (tokens, head)))[:1, :])
        g_head = g_ref[:, h * head : (h + 1) * head]
        g_rows[span, :] = g_head
        g_aug_t[:head, span] = jnp.transpose(g_head.astype(f32)).astype(bf16)
    row_factor = jnp.concatenate(row_factors, axis=1)
    g_aug_t[head:, :] = jnp.zeros((head, width), bf16)
    v_aug[:, head:] = jnp.ones((tokens, head), bf16)

    def forward(slot, key_rows, values, causal):
        codes, scales = quantize(key_rows[...].astype(f32))
        k_hat_t[slot] = jnp.transpose(codes * (scales / 127.0)).astype(bf16)
        scaled = codes * scales
        high = scaled.astype(bf16)
        low = (scaled - high.astype(f32)).astype(bf16)
        keys = jnp.concatenate([high, low], axis=1)
        values_t = jnp.transpose(values[...].astype(f32)).astype(bf16)
        for start in range(0, width, chunk):
            part = slice(start, start + chunk)
            raw = dot(keys, q_codes_t[:, part])
            if causal:
                key_at = lax.broadcasted_iota(jnp.int32, raw.shape, 0)
                query_at = lax.broadcasted_iota(jnp.int32, raw.shape, 1) + start % tokens
                raw = jnp.where(key_at <= query_at, raw, -jnp.inf)
            factor = row_factor[:, part]
            top = jnp.max(raw, axis=0, keepdims=True) * factor
            weights = jnp.exp2(raw * factor - top)
            tops[slot, :, part] = top
            sums[slot, :, part] = jnp.sum(weights, axis=0, keepdims=True)
            rounded = weights.astype(bf16)
            probs[slot, :, part] = rounded
            mixed_t[slot, :, part] = dot(values_t, rounded)

    forward(levels, k_ref, v_ref, True)

    def forward_level(level, carry):
        for source, target, send, recv in (
            (k_ref, k_in, send_k, recv_k),
            (v_ref, v_in, send_v, recv_v),
        ):
            pltpu.make_async_remote_copy(
                src_ref=source,
                dst_ref=target.at[level],
                send_sem=send.at[level],
                recv_sem=recv.at[level],
                device_id=ahead(1),
                device_id_type=MESH,
            ).wait_recv()
        forward(level, k_in.at[level], v_in.at[level], False)
        return carry

    lax.fori_loop(0, levels, forward_level, 0)

    top_list = [tops[levels]]
    for level in range(levels):
        allowed = jnp.logical_and(block_id >= 2**level, link_ref[0, level] == 1)
        top_list.append(jnp.where(allowed, tops[level], -jnp.inf))
    row_top = functools.reduce(jnp.maximum, top_list)
    shares = [jnp.exp2(top - row_top) for top in top_list]
    slots = [levels] + list(range(levels))
    total = sum(share * sums[slot] for share, slot in zip(shares, slots))
    shares = [share / total for share in shares]
    mixed = sum(share * mixed_t[slot] for share, slot in zip(shares, slots))
    for share, slot in zip(shares, slots):
        weight_ref[slot] = share
    attended_t = mixed.astype(bf16).astype(f32)
    delta = -jnp.sum(g_aug_t[:head, :].astype(f32) * attended_t, axis=0, keepdims=True)
    first = delta.astype(bf16)
    second = (delta - first.astype(f32)).astype(bf16)
    third = (delta - first.astype(f32) - second.astype(f32)).astype(bf16)
    row_at = lax.broadcasted_iota(jnp.int32, (16, width), 0)
    g_aug_t[head : head + 16, :] = jnp.where(
        row_at == 0,
        first.astype(f32),
        jnp.where(
            row_at == 1, second.astype(f32), jnp.where(row_at == 2, third.astype(f32), 0.0)
        ),
    ).astype(bf16)
    for h in range(heads):
        out_ref[:, h * head : (h + 1) * head] = jnp.transpose(
            attended_t[:, h * tokens : (h + 1) * tokens]
        ).astype(bf16)
    dq_t[...] = jnp.zeros_like(dq_t)

    def backward(slot, values):
        v_aug[:, :head] = values[...]
        for start in range(0, width, chunk):
            part = slice(start, start + chunk)
            share = weight_ref[slot, :, part].astype(bf16)
            prob = probs[slot, :, part] * share
            grad = dot(v_aug[...], g_aug_t[:, part]).astype(bf16) * prob
            probs_now[:, part] = prob
            ds_now[:, part] = grad
            dq_t[:, part] += dot(k_hat_t[slot], grad)
        return dot(ds_now[...], q_hat[...]) * score_scale, dot(probs_now[...], g_rows[...])

    def part_copy(level, kind, device):
        return pltpu.make_async_remote_copy(
            src_ref=part_out.at[level, kind],
            dst_ref=part_in.at[level, kind],
            send_sem=send_part.at[level, kind],
            recv_sem=recv_part.at[level, kind],
            device_id=device,
            device_id_type=MESH,
        )

    def backward_level(level, distance):
        key_part, value_part = backward(level, v_in.at[level])
        part_out[level, 0] = key_part.astype(bf16)
        part_out[level, 1] = value_part.astype(bf16)
        for kind in range(2):
            part_copy(level, kind, behind(distance)).start()
        return distance * 2

    lax.fori_loop(0, levels, backward_level, jnp.int32(1))
    key_sum, value_sum = backward(levels, v_ref)
    for h in range(heads):
        dq_ref[:, h * head : (h + 1) * head] = (
            jnp.transpose(dq_t[:, h * tokens : (h + 1) * tokens]) * score_scale
        ).astype(bf16)
    for level in range(levels):
        for kind in range(2):
            part_copy(level, kind, behind(2**level)).wait_recv()
        key_sum = key_sum + part_in[level, 0].astype(f32)
        value_sum = value_sum + part_in[level, 1].astype(f32)
    dk_ref[...] = key_sum.astype(bf16)
    dv_ref[...] = value_sum.astype(bf16)
    for copy in sends:
        copy.wait_send()
    for level in range(levels):
        for kind in range(2):
            part_copy(level, kind, behind(2**level)).wait_send()


def local(rows, cols, queries, key_rows, value_rows, out_grad, link_mask):
    tokens, head = key_rows.shape
    heads = queries.shape[1] // head
    levels = link_mask.shape[1]
    width = heads * tokens
    sources = levels + 1
    dma = pltpu.SemaphoreType.DMA
    vmem = pl.BlockSpec(memory_space=pltpu.VMEM)
    return pl.pallas_call(
        functools.partial(kernel, rows, cols, levels, min(256, tokens)),
        out_shape=(
            jax.ShapeDtypeStruct(queries.shape, bf16),
            jax.ShapeDtypeStruct(queries.shape, bf16),
            jax.ShapeDtypeStruct(key_rows.shape, bf16),
            jax.ShapeDtypeStruct(value_rows.shape, bf16),
        ),
        in_specs=[vmem, vmem, vmem, vmem, pl.BlockSpec(memory_space=pltpu.SMEM)],
        out_specs=(vmem, vmem, vmem, vmem),
        scratch_shapes=[
            pltpu.VMEM((levels, tokens, head), bf16),
            pltpu.VMEM((levels, tokens, head), bf16),
            pltpu.VMEM((levels, 2, tokens, head), bf16),
            pltpu.VMEM((levels, 2, tokens, head), bf16),
            pltpu.VMEM((2 * head, width), bf16),
            pltpu.VMEM((width, head), bf16),
            pltpu.VMEM((width, head), bf16),
            pltpu.VMEM((2 * head, width), bf16),
            pltpu.VMEM((sources, head, tokens), bf16),
            pltpu.VMEM((tokens, 2 * head), bf16),
            pltpu.VMEM((sources, tokens, width), bf16),
            pltpu.VMEM((sources, head, width), f32),
            pltpu.VMEM((head, width), f32),
            pltpu.VMEM((tokens, width), bf16),
            pltpu.VMEM((tokens, width), bf16),
            pltpu.VMEM((sources, 1, width), f32),
            pltpu.VMEM((sources, 1, width), f32),
            pltpu.VMEM((sources, 1, width), f32),
            dma((levels,)),
            dma((levels,)),
            dma((levels,)),
            dma((levels,)),
            dma((levels, 2)),
            dma((levels, 2)),
        ],
        compiler_params=pltpu.CompilerParams(
            collective_id=0, has_side_effects=True, vmem_limit_bytes=48 * 2**20
        ),
    )(queries, key_rows, value_rows, out_grad, link_mask)


def solution(mesh):
    spec = P(("row", "col"), None)
    return jax.shard_map(
        functools.partial(local, mesh.shape["row"], mesh.shape["col"]),
        mesh=mesh,
        in_specs=(spec,) * 5,
        out_specs=(spec,) * 4,
        check_vma=False,
    )
```

time: 169 us -> 65.6 us (0.39)
  the two profiles are of different devices: /device:TPU:30 before, /device:TPU:26 now
where the time goes in v1:
time: 65.6 us; the launch traced here: 65.5 us
  Pallas kernels  57.7 us (88%)
  local copies, waits for them, and re-layouts  7.07 us (11%)
    pallas_call x1, Pallas kernels, local(): pl.pallas_call(functools.partial(kernel, rows, cols, levels, min(256, tok...  57.7 us
    unnamed x14, local copies, waits for them, and re-layouts  7.07 us

profile of v1, /device:TPU:26, one launch (start us, length us, event | category | flops | bytes accessed | tf_op | source)
XLA Modules:
  0.0 65.5 jit_solution(13475876028925672464)
XLA Ops:
  0.6 0.0 copy-start
  0.6 0.9 %copy-done = bf16[512,256]{1,0:T(8,128)(2,1)S(1)} copy-done((bf16[512,256]{1,0:T(8,128)(2,1)S(1)}, bf16[512,256]{1,0:T(8,128)(2,1)}, u32[]{:S(2)}) %copy-start) | copy-done | bytes 262168
  1.6 0.0 copy-start.1
  1.6 0.9 %copy-done.1 = bf16[512,256]{1,0:T(8,128)(2,1)S(1)} copy-done((bf16[512,256]{1,0:T(8,128)(2,1)S(1)}, bf16[512,256]{1,0:T(8,128)(2,1)}, u32[]{:S(2)}) %copy-start.1) | copy-done | bytes 262168
  2.5 0.0 copy-start.2
  2.5 0.9 %copy-done.2 = bf16[512,128]{1,0:T(8,128)(2,1)S(1)} copy-done((bf16[512,128]{1,0:T(8,128)(2,1)S(1)}, bf16[512,128]{1,0:T(8,128)(2,1)}, u32[]{:S(2)}) %copy-start.2) | copy-done | bytes 131096
  3.4 0.0 copy-start.3
  3.4 0.9 %copy-done.3 = bf16[512,128]{1,0:T(8,128)(2,1)S(1)} copy-done((bf16[512,128]{1,0:T(8,128)(2,1)S(1)}, bf16[512,128]{1,0:T(8,128)(2,1)}, u32[]{:S(2)}) %copy-start.3) | copy-done | bytes 131096
  4.3 0.0 copy-start.4
  4.3 0.7 copy-done.4
  5.0 57.7 %shard_map.84 = (bf16[512,256]{1,0:T(8,128)(2,1)S(1)}, bf16[512,256]{1,0:T(8,128)(2,1)S(1)}, bf16[512,128]{1,0:T(8,128)(2,1)S(1)}, bf16[512,128]{1,0:T(8,128)(2,1)S(1)}) custom-call(bf16[512,256]{1,0:T(8,128)(2,1)S(1)} %copy-done, bf16[512,128]{1,0:T(8,128)(2,1)S(1)} %copy-done.2, bf16[512,128]{1,0:T(8,128)(2,1)S(1)} %copy-done.3, ...), custom_call_target="tpu_custom_call" | custom-call | tf_op jit(solution)/shard_map/pallas_call | solution.py:226
  62.7 0.7 %copy.13 = bf16[512,256]{1,0:T(8,128)(2,1)} copy(bf16[512,256]{1,0:T(8,128)(2,1)S(1)} %get-tuple-element.8) | data formatting | bytes 524288
  63.4 0.7 %copy.14 = bf16[512,256]{1,0:T(8,128)(2,1)} copy(bf16[512,256]{1,0:T(8,128)(2,1)S(1)} %get-tuple-element.9) | data formatting | bytes 524288
  64.1 0.7 %copy.15 = bf16[512,128]{1,0:T(8,128)(2,1)} copy(bf16[512,128]{1,0:T(8,128)(2,1)S(1)} %get-tuple-element.10) | data formatting | bytes 262144
  64.8 0.7 %copy.16 = bf16[512,128]{1,0:T(8,128)(2,1)} copy(bf16[512,128]{1,0:T(8,128)(2,1)S(1)} %get-tuple-element.11) | data formatting | bytes 262144
Async XLA Ops:
  0.6 1.0 %copy-start = (bf16[512,256]{1,0:T(8,128)(2,1)S(1)}, bf16[512,256]{1,0:T(8,128)(2,1)}, u32[]{:S(2)}) copy-start(bf16[512,256]{1,0:T(8,128)(2,1)} %q_ref.1) | copy-start | bytes 786436
  1.6 0.9 %copy-start.1 = (bf16[512,256]{1,0:T(8,128)(2,1)S(1)}, bf16[512,256]{1,0:T(8,128)(2,1)}, u32[]{:S(2)}) copy-start(bf16[512,256]{1,0:T(8,128)(2,1)} %g_ref.1) | copy-start | bytes 786436
  2.5 0.9 %copy-start.2 = (bf16[512,128]{1,0:T(8,128)(2,1)S(1)}, bf16[512,128]{1,0:T(8,128)(2,1)}, u32[]{:S(2)}) copy-start(bf16[512,128]{1,0:T(8,128)(2,1)} %k_ref.1) | copy-start | bytes 393220
  3.4 0.9 %copy-start.3 = (bf16[512,128]{1,0:T(8,128)(2,1)S(1)}, bf16[512,128]{1,0:T(8,128)(2,1)}, u32[]{:S(2)}) copy-start(bf16[512,128]{1,0:T(8,128)(2,1)} %v_ref.1) | copy-start | bytes 393220
  4.3 0.7 %copy-start.4 = (s32[1,5]{1,0:T(1,128)S(1)}, s32[1,5]{1,0:T(1,128)}, u32[]{:S(2)}) copy-start(s32[1,5]{1,0:T(1,128)} %link_ref.1) | copy-start | bytes 64

commit v2 on v1

v2 whole, which is shorter than its diff:
```python
import functools
import math

import jax
import jax.numpy as jnp
from jax import lax
from jax.experimental import pallas as pl
from jax.experimental.pallas import tpu as pltpu
from jax.sharding import PartitionSpec as P

scale_eps = 1e-06
MESH = pl.DeviceIdType.MESH
bf16 = jnp.bfloat16
f32 = jnp.float32
RING = 4
NEAR, TWO, GROUP, PAIR, FAR = range(5)
KEY, VALUE = 0, 1


def quantize(values):
    largest = jnp.max(jnp.abs(values), axis=1, keepdims=True)
    scales = (largest + scale_eps).astype(bf16).astype(f32)
    codes = jnp.clip(jnp.floor(values * (127.0 / scales) + 0.5), -127.0, 127.0)
    return codes, scales


def dot(left, right):
    return jnp.dot(left, right, preferred_element_type=f32)


def kernel(
    rows, cols, levels, chunk,
    q_hbm, k_hbm, v_hbm, g_hbm, link_ref,
    out_ref, dq_ref, dk_ref, dv_ref,
    q_ref, g_ref, kv, kv_in, part_out, part_in, held,
    keys, q_codes_t, q_hat, g_rows, g_aug_t, k_hat_t, values_t, scores, probs, ds, tops,
    load_sem, send_fwd, recv_fwd, send_bwd, recv_bwd,
):
    tokens, head = k_hbm.shape
    heads = q_hbm.shape[1] // head
    width = heads * tokens
    blocks = rows * cols
    block_id = lax.axis_index("row") * cols + lax.axis_index("col")
    score_scale = 1.0 / math.sqrt(head)
    in_ring = lax.rem(block_id, RING)
    ring_start = block_id - in_ring
    core = lax.rem(block_id // 8, 2)
    distances = [2**level for level in range(levels)]

    def place(block):
        return (block // cols, lax.rem(block, cols))

    def ring(steps):
        return ring_start + lax.rem(in_ring + steps, RING)

    partner = block_id + 8 - 16 * core
    ahead = [ring(1), ring(2), block_id + 4, partner, block_id + 16]
    behind = [ring(3), ring(2), block_id - 4, partner, block_id - 16]

    loads = []
    for index, (source, target) in enumerate(
        ((k_hbm, kv.at[KEY]), (v_hbm, kv.at[VALUE]), (q_hbm, q_ref), (g_hbm, g_ref))
    ):
        copy = pltpu.make_async_copy(source, target, load_sem.at[index])
        copy.start()
        loads.append(copy)

    def has_next(level):
        return block_id + distances[level] < blocks

    def has_prev(level):
        return block_id >= distances[level]

    barrier = pltpu.get_barrier_semaphore()

    def greet(block):
        pl.semaphore_signal(barrier, inc=1, device_id=place(block), device_id_type=MESH)

    for other in (ring(1), ring(2), ring(3), partner):
        greet(other)
    for level in (GROUP, FAR):
        pl.when(has_next(level))(functools.partial(greet, ahead[level]))
        pl.when(has_prev(level))(functools.partial(greet, behind[level]))

    for level in range(GROUP, levels):
        @pl.when(jnp.logical_not(has_prev(level)))
        def _():
            kv_in[level] = jnp.zeros(kv_in.shape[1:], bf16)

    for level in (GROUP, FAR):
        @pl.when(jnp.logical_not(has_next(level)))
        def _():
            part_in[level] = jnp.zeros(part_in.shape[1:], bf16)

    met = sum(has(level).astype(jnp.int32) for level in (GROUP, FAR) for has in (has_next, has_prev))
    for copy in loads[:2]:
        copy.wait()
    pl.semaphore_wait(barrier, 4 + met)

    def forward_copy(level, kind, source):
        return pltpu.make_async_remote_copy(
            src_ref=source.at[kind],
            dst_ref=kv_in.at[level, kind],
            send_sem=send_fwd.at[level, kind],
            recv_sem=recv_fwd.at[level, kind],
            device_id=place(ahead[level]),
            device_id_type=MESH,
        )

    def send_rows(condition, level, kind, source):
        @pl.when(condition)
        def _():
            forward_copy(level, kind, source).start()

    def wait_rows(level, kind):
        if level < GROUP:
            forward_copy(level, kind, kv).wait_recv()
        else:
            @pl.when(has_prev(level))
            def _():
                forward_copy(level, kind, kv).wait_recv()

    relays_pair = jnp.logical_and(core == 1, has_prev(FAR))
    for kind in (KEY, VALUE):
        send_rows(has_next(FAR), FAR, kind, kv)
        send_rows(has_next(GROUP), GROUP, kind, kv)
        send_rows(core == 0, PAIR, kind, kv)
        send_rows(in_ring < RING - 1, NEAR, kind, kv)
        send_rows(in_ring < RING - 2, TWO, kind, kv)

    def pass_far(kind):
        wait_rows(FAR, kind)
        send_rows(relays_pair, PAIR, kind, kv_in.at[FAR])

    def pass_group(kind):
        wait_rows(GROUP, kind)
        send_rows(in_ring >= RING - 1, NEAR, kind, kv_in.at[GROUP])
        send_rows(in_ring >= RING - 2, TWO, kind, kv_in.at[GROUP])

    for copy in loads[2:]:
        copy.wait()
    row_factors = []
    for h in range(heads):
        span = pl.ds(h * tokens, tokens)
        codes, scales = quantize(q_ref[:, h * head : (h + 1) * head].astype(f32))
        q_hat[span, :] = (codes * (scales / 127.0)).astype(bf16)
        codes_t = jnp.transpose(codes.astype(bf16))
        q_codes_t[:head, span] = codes_t
        q_codes_t[head:, span] = codes_t
        factor = scales * (1.0 / (127.0 * 127.0 * math.sqrt(head))) * (1.0 / math.log(2.0))
        row_factors.append(jnp.transpose(jnp.broadcast_to(factor, (tokens, head)))[:1, :])
        g_head = g_ref[:, h * head : (h + 1) * head]
        g_aug_t[:head, span] = jnp.transpose(g_head)
    row_factor = jnp.concatenate(row_factors, axis=1)
    g_aug_t[head:, :] = jnp.zeros((head, width), bf16)

    def rows_of(slot):
        return kv if slot == levels else kv_in.at[slot]

    def fold(values, reduce):
        return reduce(values.reshape(-1, 8, values.shape[1]), axis=0)

    parts = [slice(start, start + chunk) for start in range(0, width, chunk)]

    def score(slot):
        codes, scales = quantize(rows_of(slot)[KEY].astype(f32))
        span = slice(slot * tokens, (slot + 1) * tokens)
        k_hat_t[:, span] = jnp.transpose((codes * (scales / 127.0)).astype(bf16))
        scaled = codes * scales
        high = scaled.astype(bf16)
        keys[:, :head] = high
        keys[:, head:] = (scaled - high.astype(f32)).astype(bf16)
        for part in parts:
            raw = dot(keys[...], q_codes_t[:, part])
            if slot == levels:
                key_at = lax.broadcasted_iota(jnp.int32, raw.shape, 0)
                query_at = lax.broadcasted_iota(jnp.int32, raw.shape, 1) + part.start % tokens
                raw = jnp.where(key_at <= query_at, raw, -jnp.inf)
            scores[span, part] = raw
            tops[slot, :, part] = fold(raw, jnp.max)

    pass_far(KEY)
    score(levels)
    pass_group(KEY)
    score(FAR)
    pass_far(VALUE)
    score(GROUP)
    pass_group(VALUE)
    for slot in (PAIR, NEAR, TWO):
        wait_rows(slot, KEY)
        score(slot)
    for slot in (PAIR, NEAR, TWO):
        wait_rows(slot, VALUE)
    order = (PAIR, TWO, NEAR, FAR, GROUP, levels)

    allowed = [
        jnp.logical_and(has_prev(level), link_ref[0, level] == 1) for level in range(levels)
    ]
    level_tops = [jnp.max(tops[slot], axis=0, keepdims=True) for slot in range(levels + 1)]
    row_top = level_tops[levels]
    for level in range(levels):
        row_top = jnp.maximum(row_top, jnp.where(allowed[level], level_tops[level], -jnp.inf))
    row_top = row_top * row_factor

    total = jnp.zeros((8, width), f32)
    tile = 128
    for slot in order:
        factor, top = row_factor, row_top
        if slot < levels:
            factor = jnp.where(allowed[slot], factor, 0.0)
            top = jnp.where(allowed[slot], top, 1e30)
        values_t[:, slot * tokens : (slot + 1) * tokens] = jnp.transpose(rows_of(slot)[VALUE])
        sums = []
        for part in parts:
            acc = jnp.zeros((8, chunk), f32)
            for start in range(slot * tokens, (slot + 1) * tokens, tile):
                span = slice(start, start + tile)
                weights = jnp.exp2(scores[span, part] * factor[:, part] - top[:, part])
                acc = acc + fold(weights, jnp.sum)
                probs[span, part] = weights.astype(bf16)
            sums.append(acc)
        total = total + jnp.concatenate(sums, axis=1)
    scale_row = 1.0 / jnp.sum(total, axis=0, keepdims=True)
    scale_column = jnp.transpose(jnp.broadcast_to(scale_row, (head, width)))
    for h in range(heads):
        span = slice(h * tokens, (h + 1) * tokens)
        g_head = g_ref[:, h * head : (h + 1) * head].astype(f32)
        g_rows[span, :] = (g_head * scale_column[span]).astype(bf16)
    q_hat[...] = (q_hat[...].astype(f32) * (scale_column * score_scale)).astype(bf16)

    def back_copy(level, kind):
        return pltpu.make_async_remote_copy(
            src_ref=part_out.at[level, kind],
            dst_ref=part_in.at[level, kind],
            send_sem=send_bwd.at[level, kind],
            recv_sem=recv_bwd.at[level, kind],
            device_id=place(behind[level]),
            device_id_type=MESH,
        )

    def wait_part(level, kind):
        if level in (GROUP, FAR):
            @pl.when(has_next(level))
            def _():
                back_copy(level, kind).wait_recv()
        else:
            back_copy(level, kind).wait_recv()

    def chosen(condition, level, kind):
        return jnp.where(condition, part_in[level, kind].astype(f32), 0.0)

    group_sends_now = jnp.logical_and(has_prev(GROUP), in_ring < RING - 2)
    group_relays = jnp.logical_and(has_prev(GROUP), in_ring >= RING - 2)

    def give(level, kind, part):
        if level == FAR:
            wait_part(PAIR, kind)
            part = part + chosen(core == 1, PAIR, kind)
        if level == GROUP:
            held[kind] = part
        part_out[level, kind] = part.astype(bf16)
        if level in (NEAR, TWO, PAIR):
            back_copy(level, kind).start()
        else:
            @pl.when(has_prev(FAR) if level == FAR else group_sends_now)
            def _():
                back_copy(level, kind).start()

    def relay(kind):
        wait_part(NEAR, kind)
        wait_part(TWO, kind)

        @pl.when(group_relays)
        def _():
            part = held[kind] + chosen(in_ring == RING - 1, NEAR, kind) + part_in[TWO, kind].astype(f32)
            part_out[GROUP, kind] = part.astype(bf16)
            back_copy(GROUP, kind).start()

    own = [None, None]

    def all_rows(slot):
        return slice(slot * tokens, (slot + 1) * tokens)

    for slot in order:
        part = dot(probs[all_rows(slot), :], g_rows[...])
        if slot == levels:
            own[VALUE] = part
        else:
            give(slot, VALUE, part)

    attended = []
    for part in parts:
        mixed = dot(values_t[...], probs[:, part])
        attended_t = (mixed * scale_row[:, part]).astype(bf16)
        attended.append(attended_t)
        delta = -jnp.sum(
            g_aug_t[:head, part].astype(f32) * attended_t.astype(f32), axis=0, keepdims=True
        )
        first = delta.astype(bf16).astype(f32)
        second = (delta - first).astype(bf16).astype(f32)
        third = delta - first - second
        row_at = lax.broadcasted_iota(jnp.int32, (16, chunk), 0)
        pieces = jnp.where(row_at == 0, first, jnp.where(row_at == 1, second, third))
        g_aug_t[head : head + 16, part] = jnp.where(row_at < 3, pieces, 0.0).astype(bf16)

    ones = jnp.ones((tokens, head), bf16)
    for slot in order:
        v_aug = jnp.concatenate([rows_of(slot)[VALUE], ones], axis=1)
        for part in parts:
            grad = dot(v_aug, g_aug_t[:, part]).astype(bf16)
            ds[all_rows(slot), part] = grad * probs[all_rows(slot), part]
        part = dot(ds[all_rows(slot), :], q_hat[...])
        if slot == levels:
            own[KEY] = part
        else:
            give(slot, KEY, part)

    relay(VALUE)
    per_head = tokens // chunk
    for index, part in enumerate(parts):
        h = index // per_head
        rows_here = slice(part.start - h * tokens, part.stop - h * tokens)
        columns = slice(h * head, (h + 1) * head)
        grad_t = dot(k_hat_t[...], ds[:, part]) * (scale_row[:, part] * score_scale)
        dq_ref[rows_here, columns] = jnp.transpose(grad_t.astype(bf16))
        out_ref[rows_here, columns] = jnp.transpose(attended[index])
    relay(KEY)

    for kind, target in ((VALUE, dv_ref), (KEY, dk_ref)):
        for level in (GROUP, FAR):
            wait_part(level, kind)
        total_part = own[kind]
        for level, mine in (
            (NEAR, in_ring < RING - 1), (TWO, in_ring < RING - 2), (GROUP, has_next(GROUP)),
            (PAIR, core == 0), (FAR, has_next(FAR)),
        ):
            total_part = total_part + chosen(mine, level, kind)
        target[...] = total_part.astype(bf16)
    for kind in (KEY, VALUE):
        for level in range(levels):
            sent = {
                NEAR: True, TWO: True, GROUP: has_next(GROUP), FAR: has_next(FAR),
                PAIR: jnp.logical_or(core == 0, relays_pair),
            }[level]
            back = {NEAR: True, TWO: True, PAIR: True}.get(level, has_prev(level))
            for condition, copy in (
                (sent, forward_copy(level, kind, kv)), (back, back_copy(level, kind))
            ):
                if condition is True:
                    copy.wait_send()
                else:
                    pl.when(condition)(copy.wait_send)


def local(rows, cols, queries, key_rows, value_rows, out_grad, link_mask):
    tokens, head = key_rows.shape
    heads = queries.shape[1] // head
    levels = link_mask.shape[1]
    width = heads * tokens
    sources = levels + 1
    dma = pltpu.SemaphoreType.DMA
    vmem = pl.BlockSpec(memory_space=pltpu.VMEM)
    hbm = pl.BlockSpec(memory_space=pl.ANY)
    return pl.pallas_call(
        functools.partial(kernel, rows, cols, levels, min(256, tokens)),
        out_shape=(
            jax.ShapeDtypeStruct(queries.shape, bf16),
            jax.ShapeDtypeStruct(queries.shape, bf16),
            jax.ShapeDtypeStruct(key_rows.shape, bf16),
            jax.ShapeDtypeStruct(value_rows.shape, bf16),
        ),
        in_specs=[hbm, hbm, hbm, hbm, pl.BlockSpec(memory_space=pltpu.SMEM)],
        out_specs=(vmem, vmem, vmem, vmem),
        scratch_shapes=[
            pltpu.VMEM(queries.shape, bf16),
            pltpu.VMEM(queries.shape, bf16),
            pltpu.VMEM((2, tokens, head), bf16),
            pltpu.VMEM((levels, 2, tokens, head), bf16),
            pltpu.VMEM((levels, 2, tokens, head), bf16),
            pltpu.VMEM((levels, 2, tokens, head), bf16),
            pltpu.VMEM((2, tokens, head), f32),
            pltpu.VMEM((tokens, 2 * head), bf16),
            pltpu.VMEM((2 * head, width), bf16),
            pltpu.VMEM((width, head), bf16),
            pltpu.VMEM((width, head), bf16),
            pltpu.VMEM((2 * head, width), bf16),
            pltpu.VMEM((head, sources * tokens), bf16),
            pltpu.VMEM((head, sources * tokens), bf16),
            pltpu.VMEM((sources * tokens, width), f32),
            pltpu.VMEM((sources * tokens, width), bf16),
            pltpu.VMEM((sources * tokens, width), bf16),
            pltpu.VMEM((sources, 8, width), f32),
            dma((4,)),
            dma((levels, 2)),
            dma((levels, 2)),
            dma((levels, 2)),
            dma((levels, 2)),
        ],
        compiler_params=pltpu.CompilerParams(
            collective_id=0, has_side_effects=True, vmem_limit_bytes=60 * 2**20
        ),
    )(queries, key_rows, value_rows, out_grad, link_mask)


def solution(mesh):
    spec = P(("row", "col"), None)
    return jax.shard_map(
        functools.partial(local, mesh.shape["row"], mesh.shape["col"]),
        mesh=mesh,
        in_specs=(spec,) * 5,
        out_specs=(spec,) * 4,
        check_vma=False,
    )
```

time: 65.6 us -> 53.8 us (0.82)
  the two profiles are of different devices: /device:TPU:26 before, /device:TPU:30 now
where the time goes in v2:
time: 53.8 us; the launch traced here: 53.3 us
  Pallas kernels  48.3 us (90%)
  local copies, waits for them, and re-layouts  4.32 us (8%)
  between operations  0.65 us (1%)
    pallas_call x1, Pallas kernels, local(): pl.pallas_call(functools.partial(kernel, rows, cols, levels, min(256, tok...  48.3 us
    unnamed x10, local copies, waits for them, and re-layouts  4.32 us

profile of v2, /device:TPU:30, one launch (start us, length us, event | category | flops | bytes accessed | tf_op | source)
XLA Modules:
  0.0 53.3 jit_solution(14428861351803019663)
XLA Ops:
  0.6 48.3 %shard_map.84 = (bf16[512,256]{1,0:T(8,128)(2,1)}, bf16[512,256]{1,0:T(8,128)(2,1)}, bf16[512,128]{1,0:T(8,128)(2,1)}, bf16[512,128]{1,0:T(8,128)(2,1)}) custom-call(bf16[512,256]{1,0:T(8,128)(2,1)} %q_hbm.1, bf16[512,128]{1,0:T(8,128)(2,1)} %k_hbm.1, bf16[512,128]{1,0:T(8,128)(2,1)} %v_hbm.1, bf16[512,256]{1,0:T(8,128)(2,1)} %g_hbm.1, s32[1,5]{1,0:T(1,128)} %link_ref.1), custom_call_target="tpu_custom_call" | custom-call | tf_op jit(solution)/shard_map/pallas_call | solution.py:364
  49.0 0.0 copy-start
  49.0 1.7 %copy.13 = bf16[512,256]{1,0:T(8,128)(2,1)} copy(bf16[512,256]{1,0:T(8,128)(2,1)} %get-tuple-element.8) | data formatting | bytes 524288
  50.7 0.0 copy-done
  50.7 0.0 copy-start.2
  50.7 0.7 %copy.14 = bf16[512,256]{1,0:T(8,128)(2,1)} copy(bf16[512,256]{1,0:T(8,128)(2,1)S(1)} %copy-done) | data formatting | bytes 524288
  51.4 0.3 copy-done.2
  51.7 0.0 copy-start.1
  51.7 0.7 %copy.15 = bf16[512,128]{1,0:T(8,128)(2,1)} copy(bf16[512,128]{1,0:T(8,128)(2,1)S(1)} %copy-done.2) | data formatting | bytes 262144
  52.4 0.3 copy-done.1
  52.7 0.7 %copy.16 = bf16[512,128]{1,0:T(8,128)(2,1)} copy(bf16[512,128]{1,0:T(8,128)(2,1)S(1)} %copy-done.1) | data formatting | bytes 262144
Async XLA Ops:
  49.0 1.7 %copy-start = (bf16[512,256]{1,0:T(8,128)(2,1)S(1)}, bf16[512,256]{1,0:T(8,128)(2,1)}, u32[]{:S(2)}) copy-start(bf16[512,256]{1,0:T(8,128)(2,1)} %get-tuple-element.9) | copy-start | bytes 786436
  50.7 1.0 %copy-start.2 = (bf16[512,128]{1,0:T(8,128)(2,1)S(1)}, bf16[512,128]{1,0:T(8,128)(2,1)}, u32[]{:S(2)}) copy-start(bf16[512,128]{1,0:T(8,128)(2,1)} %get-tuple-element.10) | copy-start | bytes 393220
  51.7 1.0 %copy-start.1 = (bf16[512,128]{1,0:T(8,128)(2,1)S(1)}, bf16[512,128]{1,0:T(8,128)(2,1)}, u32[]{:S(2)}) copy-start(bf16[512,128]{1,0:T(8,128)(2,1)} %get-tuple-element.11) | copy-start | bytes 393220

commit v3 on v2

--- a/solution.py
+++ b/solution.py
@@ -15,6 +15,7 @@
 RING = 4
 NEAR, TWO, GROUP, PAIR, FAR = range(5)
 KEY, VALUE = 0, 1
+HALVES = 2
 
 
 def quantize(values):
@@ -32,9 +33,9 @@
     rows, cols, levels, chunk,
     q_hbm, k_hbm, v_hbm, g_hbm, link_ref,
     out_ref, dq_ref, dk_ref, dv_ref,
-    q_ref, g_ref, kv, kv_in, part_out, part_in, held,
+    q_ref, g_ref, kv, kv_in, via, part_out, part_in, held,
     keys, q_codes_t, q_hat, g_rows, g_aug_t, k_hat_t, values_t, scores, probs, ds, tops,
-    load_sem, send_fwd, recv_fwd, send_bwd, recv_bwd,
+    load_sem, send_fwd, recv_fwd, send_via, recv_via, send_hop, send_bwd, recv_bwd,
 ):
     tokens, head = k_hbm.shape
     heads = q_hbm.shape[1] // head
@@ -97,45 +98,94 @@
         copy.wait()
     pl.semaphore_wait(barrier, 4 + met)
 
-    def forward_copy(level, kind, source):
+    half = tokens // HALVES
+    pieces = [(kind, piece) for kind in (KEY, VALUE) for piece in range(HALVES)]
+
+    def forward_copy(level, kind, piece, source):
+        span = pl.ds(piece * half, half)
         return pltpu.make_async_remote_copy(
-            src_ref=source.at[kind],
-            dst_ref=kv_in.at[level, kind],
-            send_sem=send_fwd.at[level, kind],
-            recv_sem=recv_fwd.at[level, kind],
+            src_ref=source.at[kind, span],
+            dst_ref=kv_in.at[level, kind, span],
+            send_sem=send_fwd.at[level, kind, piece],
+            recv_sem=recv_fwd.at[level, kind, piece],
             device_id=place(ahead[level]),
             device_id_type=MESH,
         )
 
-    def send_rows(condition, level, kind, source):
+    def hop_copy(kind, piece, source, steps, sent):
+        span = pl.ds(piece * half, half)
+        return pltpu.make_async_remote_copy(
+            src_ref=source.at[span],
+            dst_ref=kv_in.at[TWO, kind, span],
+            send_sem=sent,
+            recv_sem=recv_fwd.at[TWO, kind, piece],
+            device_id=place(ring(steps)),
+            device_id_type=MESH,
+        )
+
+    def near_copy(piece):
+        return hop_copy(KEY, piece, kv_in.at[NEAR, KEY], 1, send_fwd.at[TWO, KEY, piece])
+
+    def last_copy(kind, piece):
+        return hop_copy(kind, piece, via.at[kind], RING - 1, send_hop.at[kind, piece])
+
+    def via_copy(kind, piece, source):
+        span = pl.ds(piece * half, half)
+        return pltpu.make_async_remote_copy(
+            src_ref=source.at[kind, span],
+            dst_ref=via.at[kind, span],
+            send_sem=send_via.at[kind, piece],
+            recv_sem=recv_via.at[kind, piece],
+            device_id=place(ring(RING - 1)),
+            device_id_type=MESH,
+        )
+
+    def pass_near(condition, piece):
         @pl.when(condition)
         def _():
-            forward_copy(level, kind, source).start()
-
-    def wait_rows(level, kind):
+            wait_rows(NEAR, KEY, piece)
+
+        @pl.when(jnp.logical_and(condition, in_ring < RING - 1))
+        def _():
+            near_copy(piece).start()
+
+    def pass_via(kind, piece):
+        @pl.when(in_ring == 1 if kind == KEY else in_ring >= 0)
+        def _():
+            via_copy(kind, piece, kv).wait_recv()
+            last_copy(kind, piece).start()
+
+    def send_rows(condition, level, kind, piece, source):
+        @pl.when(condition)
+        def _():
+            forward_copy(level, kind, piece, source).start()
+
+    def wait_rows(level, kind, piece):
         if level < GROUP:
-            forward_copy(level, kind, kv).wait_recv()
+            forward_copy(level, kind, piece, kv).wait_recv()
         else:
             @pl.when(has_prev(level))
             def _():
-                forward_copy(level, kind, kv).wait_recv()
+                forward_copy(level, kind, piece, kv).wait_recv()
 
     relays_pair = jnp.logical_and(core == 1, has_prev(FAR))
-    for kind in (KEY, VALUE):
-        send_rows(has_next(FAR), FAR, kind, kv)
-        send_rows(has_next(GROUP), GROUP, kind, kv)
-        send_rows(core == 0, PAIR, kind, kv)
-        send_rows(in_ring < RING - 1, NEAR, kind, kv)
-        send_rows(in_ring < RING - 2, TWO, kind, kv)
-
-    def pass_far(kind):
-        wait_rows(FAR, kind)
-        send_rows(relays_pair, PAIR, kind, kv_in.at[FAR])
-
-    def pass_group(kind):
-        wait_rows(GROUP, kind)
-        send_rows(in_ring >= RING - 1, NEAR, kind, kv_in.at[GROUP])
-        send_rows(in_ring >= RING - 2, TWO, kind, kv_in.at[GROUP])
+    for kind, piece in pieces:
+        send_rows(has_next(GROUP), GROUP, kind, piece, kv)
+        send_rows(has_next(FAR), FAR, kind, piece, kv)
+        if kind == VALUE:
+            pl.when(in_ring < RING - 2)(via_copy(kind, piece, kv).start)
+        send_rows(in_ring < RING - 1, NEAR, kind, piece, kv)
+        send_rows(core == 0, PAIR, kind, piece, kv)
+
+    def pass_far(kind, piece):
+        wait_rows(FAR, kind, piece)
+        send_rows(relays_pair, PAIR, kind, piece, kv_in.at[FAR])
+
+    def pass_group(kind, piece):
+        wait_rows(GROUP, kind, piece)
+        send_rows(in_ring >= RING - 1, NEAR, kind, piece, kv_in.at[GROUP])
+        late = in_ring == RING - 2 if kind == KEY else in_ring >= RING - 2
+        pl.when(late)(via_copy(kind, piece, kv_in.at[GROUP]).start)
 
     for copy in loads[2:]:
         copy.wait()
@@ -160,6 +210,9 @@
     def fold(values, reduce):
         return reduce(values.reshape(-1, 8, values.shape[1]), axis=0)
 
+    def all_rows(slot):
+        return slice(slot * tokens, (slot + 1) * tokens)
+
     parts = [slice(start, start + chunk) for start in range(0, width, chunk)]
 
     def score(slot):
@@ -179,18 +232,31 @@
             scores[span, part] = raw
             tops[slot, :, part] = fold(raw, jnp.max)
 
-    pass_far(KEY)
     score(levels)
-    pass_group(KEY)
+    early = jnp.logical_or(in_ring == 1, in_ring == 2)
+    for piece in range(HALVES):
+        pass_near(early, piece)
+    for piece in range(HALVES):
+        pass_group(KEY, piece)
+        pass_far(KEY, piece)
+    score(GROUP)
+    for piece in range(HALVES):
+        pass_near(jnp.logical_not(early), piece)
+        pass_via(KEY, piece)
+    pass_group(VALUE, 0)
+    pass_far(VALUE, 0)
     score(FAR)
-    pass_far(VALUE)
-    score(GROUP)
-    pass_group(VALUE)
-    for slot in (PAIR, NEAR, TWO):
-        wait_rows(slot, KEY)
-        score(slot)
-    for slot in (PAIR, NEAR, TWO):
-        wait_rows(slot, VALUE)
+    pass_group(VALUE, 1)
+    pass_far(VALUE, 1)
+    score(NEAR)
+    pass_via(VALUE, 0)
+    for piece in range(HALVES):
+        wait_rows(PAIR, KEY, piece)
+    score(PAIR)
+    pass_via(VALUE, 1)
+    for piece in range(HALVES):
+        wait_rows(TWO, KEY, piece)
+    score(TWO)
     order = (PAIR, TWO, NEAR, FAR, GROUP, levels)
 
     allowed = [
@@ -209,7 +275,6 @@
         if slot < levels:
             factor = jnp.where(allowed[slot], factor, 0.0)
             top = jnp.where(allowed[slot], top, 1e30)
-        values_t[:, slot * tokens : (slot + 1) * tokens] = jnp.transpose(rows_of(slot)[VALUE])
         sums = []
         for part in parts:
             acc = jnp.zeros((8, chunk), f32)
@@ -228,58 +293,61 @@
         g_rows[span, :] = (g_head * scale_column[span]).astype(bf16)
     q_hat[...] = (q_hat[...].astype(f32) * (scale_column * score_scale)).astype(bf16)
 
-    def back_copy(level, kind):
+    def back_copy(level, kind, piece):
+        span = pl.ds(piece * half, half)
         return pltpu.make_async_remote_copy(
-            src_ref=part_out.at[level, kind],
-            dst_ref=part_in.at[level, kind],
-            send_sem=send_bwd.at[level, kind],
-            recv_sem=recv_bwd.at[level, kind],
+            src_ref=part_out.at[level, kind, span],
+            dst_ref=part_in.at[level, kind, span],
+            send_sem=send_bwd.at[level, kind, piece],
+            recv_sem=recv_bwd.at[level, kind, piece],
             device_id=place(behind[level]),
             device_id_type=MESH,
         )
 
-    def wait_part(level, kind):
+    def wait_part(level, kind, piece):
         if level in (GROUP, FAR):
             @pl.when(has_next(level))
             def _():
-                back_copy(level, kind).wait_recv()
+                back_copy(level, kind, piece).wait_recv()
         else:
-            back_copy(level, kind).wait_recv()
-
-    def chosen(condition, level, kind):
-        return jnp.where(condition, part_in[level, kind].astype(f32), 0.0)
+            back_copy(level, kind, piece).wait_recv()
+
+    def chosen(condition, level, kind, span=slice(None)):
+        return jnp.where(condition, part_in[level, kind, span].astype(f32), 0.0)
 
     group_sends_now = jnp.logical_and(has_prev(GROUP), in_ring < RING - 2)
     group_relays = jnp.logical_and(has_prev(GROUP), in_ring >= RING - 2)
+    spans = [slice(piece * half, (piece + 1) * half) for piece in range(HALVES)]
 
     def give(level, kind, part):
-        if level == FAR:
-            wait_part(PAIR, kind)
-            part = part + chosen(core == 1, PAIR, kind)
         if level == GROUP:
             held[kind] = part
-        part_out[level, kind] = part.astype(bf16)
-        if level in (NEAR, TWO, PAIR):
-            back_copy(level, kind).start()
-        else:
-            @pl.when(has_prev(FAR) if level == FAR else group_sends_now)
+        for piece, span in enumerate(spans):
+            here = part[span]
+            if level == FAR:
+                wait_part(PAIR, kind, piece)
+                here = here + chosen(core == 1, PAIR, kind, span)
+            part_out[level, kind, span] = here.astype(bf16)
+            if level in (NEAR, TWO, PAIR):
+                back_copy(level, kind, piece).start()
+            else:
+                @pl.when(has_prev(FAR) if level == FAR else group_sends_now)
+                def _():
+                    back_copy(level, kind, piece).start()
+
+    def relay(kind):
+        for piece, span in enumerate(spans):
+            wait_part(TWO, kind, piece)
+            wait_part(NEAR, kind, piece)
+
+            @pl.when(group_relays)
             def _():
-                back_copy(level, kind).start()
-
-    def relay(kind):
-        wait_part(NEAR, kind)
-        wait_part(TWO, kind)
-
-        @pl.when(group_relays)
-        def _():
-            part = held[kind] + chosen(in_ring == RING - 1, NEAR, kind) + part_in[TWO, kind].astype(f32)
-            part_out[GROUP, kind] = part.astype(bf16)
-            back_copy(GROUP, kind).start()
+                part = held[kind, span] + part_in[TWO, kind, span].astype(f32)
+                part = part + chosen(in_ring == RING - 1, NEAR, kind, span)
+                part_out[GROUP, kind, span] = part.astype(bf16)
+                back_copy(GROUP, kind, piece).start()
 
     own = [None, None]
-
-    def all_rows(slot):
-        return slice(slot * tokens, (slot + 1) * tokens)
 
     for slot in order:
         part = dot(probs[all_rows(slot), :], g_rows[...])
@@ -287,6 +355,12 @@
             own[VALUE] = part
         else:
             give(slot, VALUE, part)
+
+    for slot in (PAIR, NEAR, TWO):
+        for piece in range(HALVES):
+            wait_rows(slot, VALUE, piece)
+    for slot in order:
+        values_t[:, all_rows(slot)] = jnp.transpose(rows_of(slot)[VALUE])
 
     attended = []
     for part in parts:
@@ -300,11 +374,13 @@
         second = (delta - first).astype(bf16).astype(f32)
         third = delta - first - second
         row_at = lax.broadcasted_iota(jnp.int32, (16, chunk), 0)
-        pieces = jnp.where(row_at == 0, first, jnp.where(row_at == 1, second, third))
-        g_aug_t[head : head + 16, part] = jnp.where(row_at < 3, pieces, 0.0).astype(bf16)
+        split = jnp.where(row_at == 0, first, jnp.where(row_at == 1, second, third))
+        g_aug_t[head : head + 16, part] = jnp.where(row_at < 3, split, 0.0).astype(bf16)
 
     ones = jnp.ones((tokens, head), bf16)
     for slot in order:
+        if slot == FAR:
+            relay(VALUE)
         v_aug = jnp.concatenate([rows_of(slot)[VALUE], ones], axis=1)
         for part in parts:
             grad = dot(v_aug, g_aug_t[:, part]).astype(bf16)
@@ -315,7 +391,6 @@
         else:
             give(slot, KEY, part)
 
-    relay(VALUE)
     per_head = tokens // chunk
     for index, part in enumerate(parts):
         h = index // per_head
@@ -327,29 +402,49 @@
     relay(KEY)
 
     for kind, target in ((VALUE, dv_ref), (KEY, dk_ref)):
-        for level in (GROUP, FAR):
-            wait_part(level, kind)
-        total_part = own[kind]
-        for level, mine in (
-            (NEAR, in_ring < RING - 1), (TWO, in_ring < RING - 2), (GROUP, has_next(GROUP)),
-            (PAIR, core == 0), (FAR, has_next(FAR)),
-        ):
-            total_part = total_part + chosen(mine, level, kind)
-        target[...] = total_part.astype(bf16)
-    for kind in (KEY, VALUE):
+        for piece, span in enumerate(spans):
+            for level in (GROUP, FAR):
+                wait_part(level, kind, piece)
+            total_part = own[kind][span]
+            for level, mine in (
+                (NEAR, in_ring < RING - 1), (TWO, in_ring < RING - 2), (GROUP, has_next(GROUP)),
+                (PAIR, core == 0), (FAR, has_next(FAR)),
+            ):
+                total_part = total_part + chosen(mine, level, kind, span)
+            target[span, :] = total_part.astype(bf16)
+    pair_sent = jnp.logical_or(core == 0, relays_pair)
+    for kind, piece in pieces:
         for level in range(levels):
-            sent = {
-                NEAR: True, TWO: True, GROUP: has_next(GROUP), FAR: has_next(FAR),
-                PAIR: jnp.logical_or(core == 0, relays_pair),
-            }[level]
-            back = {NEAR: True, TWO: True, PAIR: True}.get(level, has_prev(level))
+            sent = {GROUP: has_next(GROUP), FAR: has_next(FAR), PAIR: pair_sent}.get(level, True)
+            if level == TWO:
+                sent = in_ring < RING - 1 if kind == KEY else False
+            back = True if level in (NEAR, TWO, PAIR) else has_prev(level)
             for condition, copy in (
-                (sent, forward_copy(level, kind, kv)), (back, back_copy(level, kind))
+                (sent, forward_copy(level, kind, piece, kv)), (back, back_copy(level, kind, piece))
             ):
                 if condition is True:
                     copy.wait_send()
-                else:
+                elif condition is not False:
                     pl.when(condition)(copy.wait_send)
+        pl.when(in_ring == RING - 2 if kind == KEY else in_ring >= 0)(
+            via_copy(kind, piece, kv).wait_send
+        )
+        pl.when(in_ring == 1 if kind == KEY else in_ring >= 0)(last_copy(kind, piece).wait_send)
+
+
+def deliver(*refs):
+    count = (len(refs) - 2) // 3
+    sources, targets, held = refs[:count], refs[count : 2 * count], refs[2 * count : 3 * count]
+    load_sem, store_sem = refs[3 * count :]
+    loads = [pltpu.make_async_copy(sources[i], held[i], load_sem.at[i]) for i in range(count)]
+    stores = [pltpu.make_async_copy(held[i], targets[i], store_sem.at[i]) for i in range(count)]
+    for load in loads:
+        load.start()
+    for load, store in zip(loads, stores):
+        load.wait()
+        store.start()
+    for store in stores:
+        store.wait()
 
 
 def local(rows, cols, queries, key_rows, value_rows, out_grad, link_mask):
@@ -361,7 +456,7 @@
     dma = pltpu.SemaphoreType.DMA
     vmem = pl.BlockSpec(memory_space=pltpu.VMEM)
     hbm = pl.BlockSpec(memory_space=pl.ANY)
-    return pl.pallas_call(
+    results = pl.pallas_call(
         functools.partial(kernel, rows, cols, levels, min(256, tokens)),
         out_shape=(
             jax.ShapeDtypeStruct(queries.shape, bf16),
@@ -376,6 +471,7 @@
             pltpu.VMEM(queries.shape, bf16),
             pltpu.VMEM((2, tokens, head), bf16),
             pltpu.VMEM((levels, 2, tokens, head), bf16),
+            pltpu.VMEM((2, tokens, head), bf16),
             pltpu.VMEM((levels, 2, tokens, head), bf16),
             pltpu.VMEM((levels, 2, tokens, head), bf16),
             pltpu.VMEM((2, tokens, head), f32),
@@ -391,15 +487,27 @@
             pltpu.VMEM((sources * tokens, width), bf16),
             pltpu.VMEM((sources, 8, width), f32),
             dma((4,)),
-            dma((levels, 2)),
-            dma((levels, 2)),
-            dma((levels, 2)),
-            dma((levels, 2)),
+            dma((levels, 2, HALVES)),
+            dma((levels, 2, HALVES)),
+            dma((2, HALVES)),
+            dma((2, HALVES)),
+            dma((2, HALVES)),
+            dma((levels, 2, HALVES)),
+            dma((levels, 2, HALVES)),
         ],
         compiler_params=pltpu.CompilerParams(
             collective_id=0, has_side_effects=True, vmem_limit_bytes=60 * 2**20
         ),
     )(queries, key_rows, value_rows, out_grad, link_mask)
+    return pl.pallas_call(
+        deliver,
+        out_shape=tuple(jax.ShapeDtypeStruct(each.shape, each.dtype) for each in results),
+        in_specs=[hbm] * len(results),
+        out_specs=(hbm,) * len(results),
+        scratch_shapes=[pltpu.VMEM(each.shape, each.dtype) for each in results]
+        + [dma((len(results),))] * 2,
+        compiler_params=pltpu.CompilerParams(vmem_limit_bytes=60 * 2**20),
+    )(*results)
 
 
 def solution(mesh):

time: 53.8 us -> 45.7 us (0.85)
  local copies, waits for them, and re-layouts: 4.32 us -> 0 us
  Pallas kernels: 48.3 us -> 44.8 us
    pallas_call x1, Pallas kernels: 48.3 us -> 42.9 us  [local(): pl.pallas_call(functools.partial(kernel, rows, cols, levels, min(256, tok...]
    unnamed x10 -> x0, local copies, waits for them, and re-layouts: 4.32 us -> none
    pallas_call x0 -> x1, Pallas kernels: none -> 1.89 us  [local(): pl.pallas_call(deliver, out_shape=tuple((jax.ShapeDtypeStruct(each.shape,...]
where the time goes in v3:
time: 45.7 us; the launch traced here: 45.6 us
  Pallas kernels  44.8 us (98%)
  between operations  0.8 us (2%)
    pallas_call x1, Pallas kernels, local(): pl.pallas_call(functools.partial(kernel, rows, cols, levels, min(256, tok...  42.9 us
    pallas_call x1, Pallas kernels, local(): pl.pallas_call(deliver, out_shape=tuple((jax.ShapeDtypeStruct(each.shape,...  1.89 us

profile of v3, /device:TPU:30, one launch (start us, length us, event | category | flops | bytes accessed | tf_op | source)
XLA Modules:
  0.0 45.6 jit_solution(901365963965429762)
XLA Ops:
  0.6 42.9 %shard_map.84 = (bf16[512,256]{1,0:T(8,128)(2,1)}, bf16[512,256]{1,0:T(8,128)(2,1)}, bf16[512,128]{1,0:T(8,128)(2,1)}, bf16[512,128]{1,0:T(8,128)(2,1)}) custom-call(bf16[512,256]{1,0:T(8,128)(2,1)} %q_hbm.1, bf16[512,128]{1,0:T(8,128)(2,1)} %k_hbm.1, bf16[512,128]{1,0:T(8,128)(2,1)} %v_hbm.1, bf16[512,256]{1,0:T(8,128)(2,1)} %g_hbm.1, s32[1,5]{1,0:T(1,128)} %link_ref.1), custom_call_target="tpu_custom_call" | custom-call | tf_op jit(solution)/shard_map/pallas_call | solution.py:459
  43.5 1.9 %shard_map.85 = (bf16[512,256]{1,0:T(8,128)(2,1)}, bf16[512,256]{1,0:T(8,128)(2,1)}, bf16[512,128]{1,0:T(8,128)(2,1)}, bf16[512,128]{1,0:T(8,128)(2,1)}) custom-call(bf16[512,256]{1,0:T(8,128)(2,1)} %get-tuple-element.8.refs_0_, bf16[512,256]{1,0:T(8,128)(2,1)} %get-tuple-element.9.refs_1_, bf16[512,128]{1,0:T(8,128)(2,1)} %get-tuple-element.10.refs_2_, ...), custom_call_target="tpu_custom_call" | custom-call | tf_op jit(solution)/shard_map/pallas_call | solution.py:502

commit v4 on v3

--- a/solution.py
+++ b/solution.py
@@ -15,7 +15,7 @@
 RING = 4
 NEAR, TWO, GROUP, PAIR, FAR = range(5)
 KEY, VALUE = 0, 1
-HALVES = 2
+PIECES = 2
 
 
 def quantize(values):
@@ -32,10 +32,11 @@
 def kernel(
     rows, cols, levels, chunk,
     q_hbm, k_hbm, v_hbm, g_hbm, link_ref,
+    out_hbm, dq_hbm, dk_hbm, dv_hbm,
     out_ref, dq_ref, dk_ref, dv_ref,
     q_ref, g_ref, kv, kv_in, via, part_out, part_in, held,
     keys, q_codes_t, q_hat, g_rows, g_aug_t, k_hat_t, values_t, scores, probs, ds, tops,
-    load_sem, send_fwd, recv_fwd, send_via, recv_via, send_hop, send_bwd, recv_bwd,
+    load_sem, store_sem, send_fwd, recv_fwd, send_via, recv_via, send_hop, send_bwd, recv_bwd,
 ):
     tokens, head = k_hbm.shape
     heads = q_hbm.shape[1] // head
@@ -66,6 +67,13 @@
         copy.start()
         loads.append(copy)
 
+    stores = [
+        pltpu.make_async_copy(source, target, store_sem.at[index])
+        for index, (source, target) in enumerate(
+            ((out_ref, out_hbm), (dq_ref, dq_hbm), (dv_ref, dv_hbm), (dk_ref, dk_hbm))
+        )
+    ]
+
     def has_next(level):
         return block_id + distances[level] < blocks
 
@@ -77,11 +85,11 @@
     def greet(block):
         pl.semaphore_signal(barrier, inc=1, device_id=place(block), device_id_type=MESH)
 
+    for level in (FAR, GROUP):
+        pl.when(has_next(level))(functools.partial(greet, ahead[level]))
+        pl.when(has_prev(level))(functools.partial(greet, behind[level]))
     for other in (ring(1), ring(2), ring(3), partner):
         greet(other)
-    for level in (GROUP, FAR):
-        pl.when(has_next(level))(functools.partial(greet, ahead[level]))
-        pl.when(has_prev(level))(functools.partial(greet, behind[level]))
 
     for level in range(GROUP, levels):
         @pl.when(jnp.logical_not(has_prev(level)))
@@ -98,8 +106,8 @@
         copy.wait()
     pl.semaphore_wait(barrier, 4 + met)
 
-    half = tokens // HALVES
-    pieces = [(kind, piece) for kind in (KEY, VALUE) for piece in range(HALVES)]
+    half = tokens // PIECES
+    pieces = [(kind, piece) for kind in (KEY, VALUE) for piece in range(PIECES)]
 
     def forward_copy(level, kind, piece, source):
         span = pl.ds(piece * half, half)
@@ -234,27 +242,31 @@
 
     score(levels)
     early = jnp.logical_or(in_ring == 1, in_ring == 2)
-    for piece in range(HALVES):
+    for piece in range(PIECES):
         pass_near(early, piece)
-    for piece in range(HALVES):
+    for piece in range(PIECES):
         pass_group(KEY, piece)
         pass_far(KEY, piece)
     score(GROUP)
-    for piece in range(HALVES):
+    for piece in range(PIECES):
         pass_near(jnp.logical_not(early), piece)
         pass_via(KEY, piece)
-    pass_group(VALUE, 0)
-    pass_far(VALUE, 0)
+    for piece in range(PIECES // 2):
+        pass_group(VALUE, piece)
+        pass_far(VALUE, piece)
     score(FAR)
-    pass_group(VALUE, 1)
-    pass_far(VALUE, 1)
+    for piece in range(PIECES // 2, PIECES):
+        pass_group(VALUE, piece)
+        pass_far(VALUE, piece)
     score(NEAR)
-    pass_via(VALUE, 0)
-    for piece in range(HALVES):
+    for piece in range(PIECES // 2):
+        pass_via(VALUE, piece)
+    for piece in range(PIECES):
         wait_rows(PAIR, KEY, piece)
     score(PAIR)
-    pass_via(VALUE, 1)
-    for piece in range(HALVES):
+    for piece in range(PIECES // 2, PIECES):
+        pass_via(VALUE, piece)
+    for piece in range(PIECES):
         wait_rows(TWO, KEY, piece)
     score(TWO)
     order = (PAIR, TWO, NEAR, FAR, GROUP, levels)
@@ -317,7 +329,7 @@
 
     group_sends_now = jnp.logical_and(has_prev(GROUP), in_ring < RING - 2)
     group_relays = jnp.logical_and(has_prev(GROUP), in_ring >= RING - 2)
-    spans = [slice(piece * half, (piece + 1) * half) for piece in range(HALVES)]
+    spans = [slice(piece * half, (piece + 1) * half) for piece in range(PIECES)]
 
     def give(level, kind, part):
         if level == GROUP:
@@ -357,7 +369,7 @@
             give(slot, VALUE, part)
 
     for slot in (PAIR, NEAR, TWO):
-        for piece in range(HALVES):
+        for piece in range(PIECES):
             wait_rows(slot, VALUE, piece)
     for slot in order:
         values_t[:, all_rows(slot)] = jnp.transpose(rows_of(slot)[VALUE])
@@ -399,6 +411,8 @@
         grad_t = dot(k_hat_t[...], ds[:, part]) * (scale_row[:, part] * score_scale)
         dq_ref[rows_here, columns] = jnp.transpose(grad_t.astype(bf16))
         out_ref[rows_here, columns] = jnp.transpose(attended[index])
+    stores[0].start()
+    stores[1].start()
     relay(KEY)
 
     for kind, target in ((VALUE, dv_ref), (KEY, dk_ref)):
@@ -412,6 +426,7 @@
             ):
                 total_part = total_part + chosen(mine, level, kind, span)
             target[span, :] = total_part.astype(bf16)
+        stores[2 if kind == VALUE else 3].start()
     pair_sent = jnp.logical_or(core == 0, relays_pair)
     for kind, piece in pieces:
         for level in range(levels):
@@ -431,6 +446,9 @@
         )
         pl.when(in_ring == 1 if kind == KEY else in_ring >= 0)(last_copy(kind, piece).wait_send)
 
+    for store in stores:
+        store.wait()
+
 
 def deliver(*refs):
     count = (len(refs) - 2) // 3
@@ -454,7 +472,6 @@
     width = heads * tokens
     sources = levels + 1
     dma = pltpu.SemaphoreType.DMA
-    vmem = pl.BlockSpec(memory_space=pltpu.VMEM)
     hbm = pl.BlockSpec(memory_space=pl.ANY)
     results = pl.pallas_call(
         functools.partial(kernel, rows, cols, levels, min(256, tokens)),
@@ -465,8 +482,12 @@
             jax.ShapeDtypeStruct(value_rows.shape, bf16),
         ),
         in_specs=[hbm, hbm, hbm, hbm, pl.BlockSpec(memory_space=pltpu.SMEM)],
-        out_specs=(vmem, vmem, vmem, vmem),
+        out_specs=(hbm, hbm, hbm, hbm),
         scratch_shapes=[
+            pltpu.VMEM(queries.shape, bf16),
+            pltpu.VMEM(queries.shape, bf16),
+            pltpu.VMEM(key_rows.shape, bf16),
+            pltpu.VMEM(value_rows.shape, bf16),
             pltpu.VMEM(queries.shape, bf16),
             pltpu.VMEM(queries.shape, bf16),
             pltpu.VMEM((2, tokens, head), bf16),
@@ -487,13 +508,14 @@
             pltpu.VMEM((sources * tokens, width), bf16),
             pltpu.VMEM((sources, 8, width), f32),
             dma((4,)),
-            dma((levels, 2, HALVES)),
-            dma((levels, 2, HALVES)),
-            dma((2, HALVES)),
-            dma((2, HALVES)),
-            dma((2, HALVES)),
-            dma((levels, 2, HALVES)),
-            dma((levels, 2, HALVES)),
+            dma((4,)),
+            dma((levels, 2, PIECES)),
+            dma((levels, 2, PIECES)),
+            dma((2, PIECES)),
+            dma((2, PIECES)),
+            dma((2, PIECES)),
+            dma((levels, 2, PIECES)),
+            dma((levels, 2, PIECES)),
         ],
         compiler_params=pltpu.CompilerParams(
             collective_id=0, has_side_effects=True, vmem_limit_bytes=60 * 2**20

time: 45.7 us -> 45.6 us (level)
  no operation moved by 1% of the time
where the time goes in v4:
time: 45.6 us; the launch traced here: 45.4 us
  Pallas kernels  44.6 us (98%)
  between operations  0.8 us (2%)
    pallas_call x1, Pallas kernels, local(): pl.pallas_call(functools.partial(kernel, rows, cols, levels, min(256, tok...  42.7 us
    pallas_call x1, Pallas kernels, local(): pl.pallas_call(deliver, out_shape=tuple((jax.ShapeDtypeStruct(each.shape,...  1.89 us

profile of v4, /device:TPU:30, one launch (start us, length us, event | category | flops | bytes accessed | tf_op | source)
XLA Modules:
  0.0 45.4 jit_solution(4273969959661523177)
XLA Ops:
  0.6 42.7 %shard_map.84 = (bf16[512,256]{1,0:T(8,128)(2,1)}, bf16[512,256]{1,0:T(8,128)(2,1)}, bf16[512,128]{1,0:T(8,128)(2,1)}, bf16[512,128]{1,0:T(8,128)(2,1)}) custom-call(bf16[512,256]{1,0:T(8,128)(2,1)} %q_hbm.1, bf16[512,128]{1,0:T(8,128)(2,1)} %k_hbm.1, bf16[512,128]{1,0:T(8,128)(2,1)} %v_hbm.1, bf16[512,256]{1,0:T(8,128)(2,1)} %g_hbm.1, s32[1,5]{1,0:T(1,128)} %link_ref.1), custom_call_target="tpu_custom_call" | custom-call | tf_op jit(solution)/shard_map/pallas_call | solution.py:476
  43.4 1.9 %shard_map.85 = (bf16[512,256]{1,0:T(8,128)(2,1)}, bf16[512,256]{1,0:T(8,128)(2,1)}, bf16[512,128]{1,0:T(8,128)(2,1)}, bf16[512,128]{1,0:T(8,128)(2,1)}) custom-call(bf16[512,256]{1,0:T(8,128)(2,1)} %get-tuple-element.8.refs_0_, bf16[512,256]{1,0:T(8,128)(2,1)} %get-tuple-element.9.refs_1_, bf16[512,128]{1,0:T(8,128)(2,1)} %get-tuple-element.10.refs_2_, ...), custom_call_target="tpu_custom_call" | custom-call | tf_op jit(solution)/shard_map/pallas_call | solution.py:524

commit v5 on v4

--- a/solution.py
+++ b/solution.py
@@ -248,11 +248,12 @@
         pass_group(KEY, piece)
         pass_far(KEY, piece)
     score(GROUP)
+    for piece in range(PIECES // 2):
+        pass_group(VALUE, piece)
     for piece in range(PIECES):
         pass_near(jnp.logical_not(early), piece)
         pass_via(KEY, piece)
     for piece in range(PIECES // 2):
-        pass_group(VALUE, piece)
         pass_far(VALUE, piece)
     score(FAR)
     for piece in range(PIECES // 2, PIECES):

time: 45.6 us -> 45.5 us (level)
  no operation moved by 1% of the time
where the time goes in v5:
time: 45.5 us; the launch traced here: 45.4 us
  Pallas kernels  44.6 us (98%)
  between operations  0.8 us (2%)
    pallas_call x1, Pallas kernels, local(): pl.pallas_call(functools.partial(kernel, rows, cols, levels, min(256, tok...  42.7 us
    pallas_call x1, Pallas kernels, local(): pl.pallas_call(deliver, out_shape=tuple((jax.ShapeDtypeStruct(each.shape,...  1.89 us

profile of v5, /device:TPU:30, one launch (start us, length us, event | category | flops | bytes accessed | tf_op | source)
XLA Modules:
  0.0 45.4 jit_solution(10609941709267650265)
XLA Ops:
  0.6 42.7 %shard_map.84 = (bf16[512,256]{1,0:T(8,128)(2,1)}, bf16[512,256]{1,0:T(8,128)(2,1)}, bf16[512,128]{1,0:T(8,128)(2,1)}, bf16[512,128]{1,0:T(8,128)(2,1)}) custom-call(bf16[512,256]{1,0:T(8,128)(2,1)} %q_hbm.1, bf16[512,128]{1,0:T(8,128)(2,1)} %k_hbm.1, bf16[512,128]{1,0:T(8,128)(2,1)} %v_hbm.1, bf16[512,256]{1,0:T(8,128)(2,1)} %g_hbm.1, s32[1,5]{1,0:T(1,128)} %link_ref.1), custom_call_target="tpu_custom_call" | custom-call | tf_op jit(solution)/shard_map/pallas_call | solution.py:477
  43.3 1.9 %shard_map.85 = (bf16[512,256]{1,0:T(8,128)(2,1)}, bf16[512,256]{1,0:T(8,128)(2,1)}, bf16[512,128]{1,0:T(8,128)(2,1)}, bf16[512,128]{1,0:T(8,128)(2,1)}) custom-call(bf16[512,256]{1,0:T(8,128)(2,1)} %get-tuple-element.8.refs_0_, bf16[512,256]{1,0:T(8,128)(2,1)} %get-tuple-element.9.refs_1_, bf16[512,128]{1,0:T(8,128)(2,1)} %get-tuple-element.10.refs_2_, ...), custom_call_target="tpu_custom_call" | custom-call | tf_op jit(solution)/shard_map/pallas_call | solution.py:525
